TPU v7x, 256 devices: a whole 4x4x8 slice. The times are simulated.
256 devices in a mesh: slab: 16 (over y, z_lo, core), spec: 16 (over x, z_hi).
Axes of the slice: x: 4, y: 4, z: 8 (z_hi: 4, z_lo: 2; z = z_hi * 2 + z_lo), core: 2. Of those that a mesh axis runs over, the one named last changes fastest.
Arguments:
- concentration: bfloat16 [256, 128, 16, 128], P('spec', 'slab'), may hold values from 0.049804688 to 2
- inhibit: bfloat16 [256, 256], replicated, may hold values from 0 to 0.015625
- priming: bfloat16 [256, 256], replicated, may hold values from 0 to 0.0077819824
- produce: bfloat16 [256, 256], replicated, may hold values from 0 to 0.0059814453
- max_rate: float32 [256], replicated, may hold values from 0.05 to 1
- half_saturation: float32 [256], replicated, may hold values from 0.2 to 2
- exudate: float32 [256], replicated, may hold values from 0.01 to 0.5
- sorption_capacity: float32 [8, 256], replicated, may hold values from 1 to 40
- sorption_affinity: float32 [8, 256], replicated, may hold values from 0.005 to 0.05
- tortuosity: float32 [8], replicated, may hold values from 0.2 to 1
- diffusivity: float32 [256], P('spec'), may hold values from 0.01 to 0.08
- velocity: float32 [128, 16, 128], P('slab'), may hold values from 0.1 to 0.5
- material: int32 [128, 16, 128], P('slab'), may hold values from 0 to 7
- root_mask: int32 [128, 16, 128], P('slab'), may hold values 0 or 1
Outputs:
- concentration_out: bfloat16 [256, 128, 16, 128], P('spec', 'slab')
All inputs are finite; a program needn't handle non-finite values. No bound on the sum of `root_mask` on one device may be relied on, other than what follows from the above.
Results may differ from a plain program's by a relative error of at most 0.0007.
The roundings to bfloat16 on the way count: a program that leaves them out, or rounds other values in their place, can miss the bound.
Values may be sent and summed in bfloat16 or wider, within the bound.
A program may use at most 64 MiB of HBM per device.

v0:
```python
import jax
import jax.numpy as jnp
from jax import lax
from jax.sharding import PartitionSpec as P

SUB = 4
STEPS = 2


def extended(block, sides, width):
    for axis, dim in sides:
        count = lax.axis_size(axis)
        forward = [(i, i + 1) for i in range(count - 1)]
        backward = [(target, source) for source, target in forward]
        low = lax.ppermute(
            lax.slice_in_dim(block, block.shape[dim] - width, None, axis=dim), axis, forward
        )
        high = lax.ppermute(lax.slice_in_dim(block, 0, width, axis=dim), axis, backward)
        block = jnp.concatenate([low, block, high], axis=dim)
    return block


def pick_by_material(values_table, labels, trailing):
    summed = None
    for material_id in range(values_table.shape[0]):
        entry = values_table[material_id].reshape(values_table.shape[1:] + (1,) * trailing)
        term = jnp.where(labels == material_id, entry, jnp.zeros((), jnp.float32))
        summed = term if summed is None else summed + term
    return summed


def divergence(mobile_padded, flow_padded, tort_padded, spread_rate):
    face_z = 0.5 * (tort_padded[:-1] + tort_padded[1:])
    flux_z = flow_padded[:-1] * mobile_padded[..., :-1, :, :] - spread_rate * face_z * (
        mobile_padded[..., 1:, :, :] - mobile_padded[..., :-1, :, :]
    )
    change = flux_z[..., :-1, :, :] - flux_z[..., 1:, :, :]
    mobile = mobile_padded[..., 1:-1, :, :]
    tortuous = tort_padded[1:-1]
    lead = [(0, 0)] * (mobile.ndim - 2)
    mobile_y = jnp.pad(mobile, lead + [(1, 1), (0, 0)])
    tort_y = jnp.pad(tortuous, ((0, 0), (1, 1), (0, 0)))
    face_y = 0.5 * (tort_y[:, :-1] + tort_y[:, 1:])
    flux_y = -spread_rate * face_y * (mobile_y[..., 1:, :] - mobile_y[..., :-1, :])
    change = change + flux_y[..., :-1, :] - flux_y[..., 1:, :]
    mobile_x = jnp.pad(mobile, lead + [(0, 0), (1, 1)])
    tort_x = jnp.pad(tortuous, ((0, 0), (0, 0), (1, 1)))
    face_x = 0.5 * (tort_x[:, :, :-1] + tort_x[:, :, 1:])
    flux_x = -spread_rate * face_x * (mobile_x[..., 1:] - mobile_x[..., :-1])
    change = change + flux_x[..., :-1] - flux_x[..., 1:]
    return change


def reaction(
    gathered,
    inhibit,
    priming,
    produce,
    max_rate,
    half_saturation,
    source_term,
    onehot,
    sorption_affinity,
):
    inhibition = jnp.dot(inhibit, gathered, preferred_element_type=jnp.float32)
    boost = jnp.dot(priming, gathered, preferred_element_type=jnp.float32)
    dissolved = gathered.astype(jnp.float32)
    rate_term = (
        max_rate[:, None] * (1.0 + boost) / (half_saturation[:, None] + dissolved + inhibition)
    )
    remaining = dissolved * jnp.exp(-rate_term)
    consumed = (dissolved - remaining).astype(jnp.bfloat16)
    reacted = (
        remaining + jnp.dot(produce, consumed, preferred_element_type=jnp.float32) + source_term
    )
    sorbed_sums = jnp.dot(sorption_affinity, reacted, precision=lax.Precision.HIGHEST)
    denominator = 1.0 + jnp.sum(onehot * sorbed_sums, axis=0)
    return (reacted.astype(jnp.bfloat16), denominator)


def body(
    concentration,
    inhibit,
    priming,
    produce,
    max_rate,
    half_saturation,
    exudate,
    sorption_capacity,
    sorption_affinity,
    tortuosity,
    diffusivity,
    velocity,
    material,
    root_mask,
):
    groups = lax.axis_size("spec")
    spec_rank = lax.axis_index("spec")
    blocks, slab_depth, plane_rows, plane_cols = concentration.shape
    species = inhibit.shape[0]
    materials = tortuosity.shape[0]
    band_rows = plane_rows // groups
    row_start = spec_rank * band_rows
    band_labels = lax.dynamic_slice_in_dim(material, row_start, band_rows, 1).reshape(-1)
    band_roots = (
        lax.dynamic_slice_in_dim(root_mask, row_start, band_rows, 1).reshape(-1).astype(jnp.float32)
    )
    onehot = (band_labels[None, :] == jnp.arange(materials, dtype=jnp.int32)[:, None]).astype(
        jnp.float32
    )
    source_term = exudate[:, None] * band_roots[None, :]
    uptake_local = lax.dynamic_slice_in_dim(
        sorption_capacity * sorption_affinity, spec_rank * blocks, blocks, 1
    )
    tort_cells = pick_by_material(tortuosity, material, 0)
    spread_rate = diffusivity.reshape(blocks, 1, 1, 1)
    ratio = pick_by_material(uptake_local, material, 3)
    rim_width = 1
    for repeat in range(STEPS):
        gathered = lax.all_to_all(concentration, "spec", split_axis=2, concat_axis=0, tiled=True)
        renewed, band_denominator = reaction(
            gathered.reshape(species, -1),
            inhibit,
            priming,
            produce,
            max_rate,
            half_saturation,
            source_term,
            onehot,
            sorption_affinity,
        )
        returned = lax.all_to_all(
            renewed.reshape(species, slab_depth, band_rows, plane_cols),
            "spec",
            split_axis=0,
            concat_axis=2,
            tiled=True,
        )
        denominator = lax.all_gather(
            band_denominator.reshape(slab_depth, band_rows, plane_cols), "spec", axis=1, tiled=True
        )
        field = returned.astype(jnp.float32)
        coefficients = jnp.stack([velocity, tort_cells])
        padded = extended(coefficients, (("slab", 1),), rim_width)
        mobile_share = 1.0 / (1.0 + ratio / denominator)
        for substep in range(SUB):
            mobile_padded = extended(mobile_share * field, (("slab", 1),), 1)
            field = field + divergence(mobile_padded, padded[0], padded[1], spread_rate)
        concentration = field.astype(jnp.bfloat16)
    return concentration


def solution(mesh):
    in_specs = (
        P("spec", "slab", None, None),
        P(),
        P(),
        P(),
        P(),
        P(),
        P(),
        P(),
        P(),
        P(),
        P("spec"),
        P("slab", None, None),
        P("slab", None, None),
        P("slab", None, None),
    )
    out_specs = P("spec", "slab", None, None)
    return jax.shard_map(body, mesh=mesh, in_specs=in_specs, out_specs=out_specs, check_vma=False)
```

profile of v0, /device:TPU:16, one launch (start us, length us, event | category | flops | bytes accessed | tf_op | source)
XLA Modules:
  0.0 258.9 jit_solution(15030759355032033949)
XLA Ops:
  2.2 11.0 %all-to-all-start = ((bf16[16,8,16,128]{3,1,0,2:T(8,128)(2,1)}), bf16[16,8,16,128]{3,1,0,2:T(8,128)(2,1)S(1)}, u32[]{:S(2)}, u32[]{:S(2)}) async-start(bf16[16,8,16,128]{3,1,0,2:T(8,128)(2,1)} %copy.39), calls=%async_computation | async-start | bytes 1048576 | tf_op jit(solution)/shard_map/all_to_all | solution.py:120
  13.9 5.1 %select_add_fusion.1 = (f32[8,16,128]{2,1,0:T(8,128)S(1)}, pred[8,16,128]{2,1,0:T(8,128)(4,1)S(1)}, pred[8,16,128]{2,1,0:T(8,128)(4,1)S(1)}, pred[8,16,128]{2,1,...) fusion(f32[]{:T(128)} %bitcast.17, f32[]{:T(128)} %bitcast.16, ...), kind=kLoop, calls=%fused_computation.222 | loop fusion | flops 376832 | bytes 262176 | tf_op jit(solution)/shard_map/add | solution.py:28
  21.0 4.5 %collective-permute-start.2 = (f32[2,1,16,128]{3,2,1,0:T(8,128)S(1)}, f32[2,1,16,128]{3,2,1,0:T(8,128)S(1)}, u32[]{:S(2)}, u32[]{:S(2)}) collective-permute-start(f32[2,1,16,128]{3,2,1,0:T(8,128)S(1)} %get-tuple-element.45), channel_id=1, source_target_pairs={{16,0},{32,16},{48,32},{64,48},{80,64},{96,80},{112,96},{128,112},... | collective-permute-start | bytes 49160 | tf_op jit(solution)/shard_map/ppermute | solution.py:18
  26.4 5.7 %all-to-all-done = bf16[16,8,16,128]{3,1,0,2:T(8,128)(2,1)S(1)} async-done(((bf16[16,8,16,128]{3,1,0,2:T(8,128)(2,1)}), bf16[16,8,16,128]{3,1,0,2:T(8,128)(2,1)S(1)}, u32[]{:S(2)}, u32[]{:S(2)}) %all-to-all-start) | async-done | bytes 524320 | tf_op jit(solution)/shard_map/all_to_all | solution.py:120
  34.7 3.9 %all-to-all-start.1 = ((bf16[256,8,1,128]{3,1,2,0:T(8,128)(2,1)}), bf16[256,8,1,128]{3,1,2,0:T(8,128)(2,1)S(1)}, u32[]{:S(2)}, u32[]{:S(2)}) async-start(bf16[256,8,1,128]{3,1,2,0:T(8,128)(2,1)} %bitcast.4), calls=%async_computation.1 | async-start | bytes 1048576 | tf_op jit(solution)/shard_map/all_to_all | solution.py:132
  39.9 47.6 %all_gather.6 = f32[8,16,128]{2,0,1:T(8,128)S(1)} all-gather(f32[8,1,128]{2,0,1:T(8,128)S(1)} %add_bitcast_fusion.1), channel_id=1, replica_groups=mesh['slab'=16,'spec'=16] {'spec'}, dimensions={1}, use_global_device_ids=true | all-gather | bytes 69632 | tf_op jit(solution)/shard_map/all_gather | solution.py:139
  91.0 2.4 collective-permute-start.1
  94.3 3.9 %collective-permute-done.1 = f32[16,1,16,128]{3,1,0,2:T(1,128)S(1)} collective-permute-done((f32[16,1,16,128]{3,1,0,2:T(1,128)S(1)}, f32[16,1,16,128]{3,1,0,2:T(1,128)S(1)}, u32[]{:S(2)}, u32[]{:S(2)}) %collective-permute-start.1) | collective-permute-done | bytes 131104 | tf_op jit(solution)/shard_map/ppermute | solution.py:15
  103.3 2.6 collective-permute-start.4
  106.2 4.3 %collective-permute-done.4 = f32[16,1,16,128]{3,1,0,2:T(1,128)S(1)} collective-permute-done((f32[16,1,16,128]{3,1,0,2:T(1,128)S(1)}, f32[16,1,16,128]{3,1,0,2:T(1,128)S(1)}, u32[]{:S(2)}, u32[]{:S(2)}) %collective-permute-start.4) | collective-permute-done | bytes 131104 | tf_op jit(solution)/shard_map/ppermute | solution.py:15
  115.6 2.4 collective-permute-start.6
  118.3 4.5 %collective-permute-done.6 = f32[16,1,16,128]{3,1,0,2:T(1,128)S(1)} collective-permute-done((f32[16,1,16,128]{3,1,0,2:T(1,128)S(1)}, f32[16,1,16,128]{3,1,0,2:T(1,128)S(1)}, u32[]{:S(2)}, u32[]{:S(2)}) %collective-permute-start.6) | collective-permute-done | bytes 131104 | tf_op jit(solution)/shard_map/ppermute | solution.py:15
  127.8 2.4 collective-permute-start.8
  130.5 4.5 %collective-permute-done.8 = f32[16,1,16,128]{3,1,0,2:T(1,128)S(1)} collective-permute-done((f32[16,1,16,128]{3,1,0,2:T(1,128)S(1)}, f32[16,1,16,128]{3,1,0,2:T(1,128)S(1)}, u32[]{:S(2)}, u32[]{:S(2)}) %collective-permute-start.8) | collective-permute-done | bytes 131104 | tf_op jit(solution)/shard_map/ppermute | solution.py:15
  136.2 19.7 %all_to_all.48 = bf16[16,8,16,128]{3,1,0,2:T(8,128)(2,1)S(1)} all-to-all(bf16[16,8,16,128]{3,1,0,2:T(8,128)(2,1)S(1)} %fusion.66), channel_id=1, replica_groups=mesh['slab'=16,'spec'=16] {'spec'}, dimensions={2} | all-to-all | bytes 1048576 | tf_op jit(solution)/shard_map/all_to_all | solution.py:120
  158.1 3.6 %all-to-all-start.3 = ((bf16[256,8,1,128]{3,1,2,0:T(8,128)(2,1)}), bf16[256,8,1,128]{3,1,2,0:T(8,128)(2,1)S(1)}, u32[]{:S(2)}, u32[]{:S(2)}) async-start(bf16[256,8,1,128]{3,1,2,0:T(8,128)(2,1)} %bitcast.39), calls=%async_computation.3 | async-start | bytes 1048576 | tf_op jit(solution)/shard_map/all_to_all | solution.py:132
  162.3 46.0 %all_gather.7 = f32[8,16,128]{2,0,1:T(8,128)S(1)} all-gather(f32[8,1,128]{2,0,1:T(8,128)S(1)} %add_bitcast_fusion), channel_id=1, replica_groups=mesh['slab'=16,'spec'=16] {'spec'}, dimensions={1}, use_global_device_ids=true | all-gather | bytes 69632 | tf_op jit(solution)/shard_map/all_gather | solution.py:139
  212.5 2.4 collective-permute-start.10
  215.2 4.5 %collective-permute-done.10 = f32[16,1,16,128]{3,1,0,2:T(1,128)S(1)} collective-permute-done((f32[16,1,16,128]{3,1,0,2:T(1,128)S(1)}, f32[16,1,16,128]{3,1,0,2:T(1,128)S(1)}, u32[]{:S(2)}, u32[]{:S(2)}) %collective-permute-start.10) | collective-permute-done | bytes 131104 | tf_op jit(solution)/shard_map/ppermute | solution.py:15
  224.8 2.4 collective-permute-start.12
  227.5 4.5 %collective-permute-done.12 = f32[16,1,16,128]{3,1,0,2:T(1,128)S(1)} collective-permute-done((f32[16,1,16,128]{3,1,0,2:T(1,128)S(1)}, f32[16,1,16,128]{3,1,0,2:T(1,128)S(1)}, u32[]{:S(2)}, u32[]{:S(2)}) %collective-permute-start.12) | collective-permute-done | bytes 131104 | tf_op jit(solution)/shard_map/ppermute | solution.py:15
  237.1 2.7 %collective-permute-start.14 = (f32[16,1,16,128]{3,1,0,2:T(1,128)S(1)}, f32[16,1,16,128]{3,1,0,2:T(1,128)S(1)}, u32[]{:S(2)}, u32[]{:S(2)}) collective-permute-start(f32[16,1,16,128]{3,1,0,2:T(1,128)S(1)} %get-tuple-element.29), channel_id=1, source_target_pairs={{0,16},{16,32},{32,48},{48,64},{64,80},{80,96},{96,112},{112,128},... | collective-permute-start | bytes 393224 | tf_op jit(solution)/shard_map/ppermute | solution.py:15
  240.0 4.3 %collective-permute-done.14 = f32[16,1,16,128]{3,1,0,2:T(1,128)S(1)} collective-permute-done((f32[16,1,16,128]{3,1,0,2:T(1,128)S(1)}, f32[16,1,16,128]{3,1,0,2:T(1,128)S(1)}, u32[]{:S(2)}, u32[]{:S(2)}) %collective-permute-start.14) | collective-permute-done | bytes 131104 | tf_op jit(solution)/shard_map/ppermute | solution.py:15
  252.0 4.5 %collective-permute-done.16 = f32[16,1,16,128]{3,1,0,2:T(1,128)S(1)} collective-permute-done((f32[16,1,16,128]{3,1,0,2:T(1,128)S(1)}, f32[16,1,16,128]{3,1,0,2:T(1,128)S(1)}, u32[]{:S(2)}, u32[]{:S(2)}) %collective-permute-start.16) | collective-permute-done | bytes 131104 | tf_op jit(solution)/shard_map/ppermute | solution.py:15
  (128 shorter events, 58.2 us)
Async XLA Ops:
  0.0 32.2 %copy-start = (bf16[256,256]{1,0:T(8,128)(2,1)S(1)}, bf16[256,256]{1,0:T(8,128)(2,1)}, u32[]{:S(2)}) copy-start(bf16[256,256]{1,0:T(8,128)(2,1)} %param.16) | copy-start | bytes 393220
  0.1 32.4 %copy-start.12 = (f32[256]{0:T(256)S(1)}, f32[256]{0:T(256)}, u32[]{:S(2)}) copy-start(f32[256]{0:T(256)} %param.19) | copy-start | bytes 3076
  0.1 32.4 %copy-start.11 = (bf16[256,256]{1,0:T(8,128)(2,1)S(1)}, bf16[256,256]{1,0:T(8,128)(2,1)}, u32[]{:S(2)}) copy-start(bf16[256,256]{1,0:T(8,128)(2,1)} %param.15) | copy-start | bytes 393220
  2.2 30.0 %all-to-all-start = ((bf16[16,8,16,128]{3,1,0,2:T(8,128)(2,1)}), bf16[16,8,16,128]{3,1,0,2:T(8,128)(2,1)S(1)}, u32[]{:S(2)}, u32[]{:S(2)}) async-start(bf16[16,8,16,128]{3,1,0,2:T(8,128)(2,1)} %copy.39), calls=%async_computation | async-start | bytes 1048576 | tf_op jit(solution)/shard_map/all_to_all | solution.py:120
  19.1 20.0 %collective-permute-start = (f32[2,1,16,128]{3,2,1,0:T(8,128)S(1)}, f32[2,1,16,128]{3,2,1,0:T(8,128)S(1)}, u32[]{:S(2)}, u32[]{:S(2)}) collective-permute-start(f32[2,1,16,128]{3,2,1,0:T(8,128)S(1)} %get-tuple-element.44), channel_id=1, source_target_pairs={{0,16},{16,32},{32,48},{48,64},{64,80},{80,96},{96,112},{112,128},... | collective-permute-start | bytes 49160 | tf_op jit(solution)/shard_map/ppermute | solution.py:15
  21.0 18.1 %collective-permute-start.2 = (f32[2,1,16,128]{3,2,1,0:T(8,128)S(1)}, f32[2,1,16,128]{3,2,1,0:T(8,128)S(1)}, u32[]{:S(2)}, u32[]{:S(2)}) collective-permute-start(f32[2,1,16,128]{3,2,1,0:T(8,128)S(1)} %get-tuple-element.45), channel_id=1, source_target_pairs={{16,0},{32,16},{48,32},{64,48},{80,64},{96,80},{112,96},{128,112},... | collective-permute-start | bytes 49160 | tf_op jit(solution)/shard_map/ppermute | solution.py:18
  34.7 52.8 %all-to-all-start.1 = ((bf16[256,8,1,128]{3,1,2,0:T(8,128)(2,1)}), bf16[256,8,1,128]{3,1,2,0:T(8,128)(2,1)S(1)}, u32[]{:S(2)}, u32[]{:S(2)}) async-start(bf16[256,8,1,128]{3,1,2,0:T(8,128)(2,1)} %bitcast.4), calls=%async_computation.1 | async-start | bytes 1048576 | tf_op jit(solution)/shard_map/all_to_all | solution.py:132
  89.1 5.2 %collective-permute-start.3 = (f32[16,1,16,128]{3,1,0,2:T(1,128)S(1)}, f32[16,1,16,128]{3,1,0,2:T(1,128)S(1)}, u32[]{:S(2)}, u32[]{:S(2)}) collective-permute-start(f32[16,1,16,128]{3,1,0,2:T(1,128)S(1)} %get-tuple-element.40), channel_id=1, source_target_pairs={{16,0},{32,16},{48,32},{64,48},{80,64},{96,80},{112,96},{128,112},... | collective-permute-start | bytes 393224 | tf_op jit(solution)/shard_map/ppermute | solution.py:18
  91.0 7.2 %collective-permute-start.1 = (f32[16,1,16,128]{3,1,0,2:T(1,128)S(1)}, f32[16,1,16,128]{3,1,0,2:T(1,128)S(1)}, u32[]{:S(2)}, u32[]{:S(2)}) collective-permute-start(f32[16,1,16,128]{3,1,0,2:T(1,128)S(1)} %get-tuple-element.41), channel_id=1, source_target_pairs={{0,16},{16,32},{32,48},{48,64},{64,80},{80,96},{96,112},{112,128},... | collective-permute-start | bytes 393224 | tf_op jit(solution)/shard_map/ppermute | solution.py:15
  101.4 4.8 %collective-permute-start.5 = (f32[16,1,16,128]{3,1,0,2:T(1,128)S(1)}, f32[16,1,16,128]{3,1,0,2:T(1,128)S(1)}, u32[]{:S(2)}, u32[]{:S(2)}) collective-permute-start(f32[16,1,16,128]{3,1,0,2:T(1,128)S(1)} %get-tuple-element.38), channel_id=1, source_target_pairs={{16,0},{32,16},{48,32},{64,48},{80,64},{96,80},{112,96},{128,112},... | collective-permute-start | bytes 393224 | tf_op jit(solution)/shard_map/ppermute | solution.py:18
  103.3 7.2 %collective-permute-start.4 = (f32[16,1,16,128]{3,1,0,2:T(1,128)S(1)}, f32[16,1,16,128]{3,1,0,2:T(1,128)S(1)}, u32[]{:S(2)}, u32[]{:S(2)}) collective-permute-start(f32[16,1,16,128]{3,1,0,2:T(1,128)S(1)} %get-tuple-element.39), channel_id=1, source_target_pairs={{0,16},{16,32},{32,48},{48,64},{64,80},{80,96},{96,112},{112,128},... | collective-permute-start | bytes 393224 | tf_op jit(solution)/shard_map/ppermute | solution.py:15
  113.7 4.6 %collective-permute-start.7 = (f32[16,1,16,128]{3,1,0,2:T(1,128)S(1)}, f32[16,1,16,128]{3,1,0,2:T(1,128)S(1)}, u32[]{:S(2)}, u32[]{:S(2)}) collective-permute-start(f32[16,1,16,128]{3,1,0,2:T(1,128)S(1)} %get-tuple-element.36), channel_id=1, source_target_pairs={{16,0},{32,16},{48,32},{64,48},{80,64},{96,80},{112,96},{128,112},... | collective-permute-start | bytes 393224 | tf_op jit(solution)/shard_map/ppermute | solution.py:18
  115.6 7.2 %collective-permute-start.6 = (f32[16,1,16,128]{3,1,0,2:T(1,128)S(1)}, f32[16,1,16,128]{3,1,0,2:T(1,128)S(1)}, u32[]{:S(2)}, u32[]{:S(2)}) collective-permute-start(f32[16,1,16,128]{3,1,0,2:T(1,128)S(1)} %get-tuple-element.37), channel_id=1, source_target_pairs={{0,16},{16,32},{32,48},{48,64},{64,80},{80,96},{96,112},{112,128},... | collective-permute-start | bytes 393224 | tf_op jit(solution)/shard_map/ppermute | solution.py:15
  125.9 4.6 %collective-permute-start.9 = (f32[16,1,16,128]{3,1,0,2:T(1,128)S(1)}, f32[16,1,16,128]{3,1,0,2:T(1,128)S(1)}, u32[]{:S(2)}, u32[]{:S(2)}) collective-permute-start(f32[16,1,16,128]{3,1,0,2:T(1,128)S(1)} %get-tuple-element.34), channel_id=1, source_target_pairs={{16,0},{32,16},{48,32},{64,48},{80,64},{96,80},{112,96},{128,112},... | collective-permute-start | bytes 393224 | tf_op jit(solution)/shard_map/ppermute | solution.py:18
  127.8 7.2 %collective-permute-start.8 = (f32[16,1,16,128]{3,1,0,2:T(1,128)S(1)}, f32[16,1,16,128]{3,1,0,2:T(1,128)S(1)}, u32[]{:S(2)}, u32[]{:S(2)}) collective-permute-start(f32[16,1,16,128]{3,1,0,2:T(1,128)S(1)} %get-tuple-element.35), channel_id=1, source_target_pairs={{0,16},{16,32},{32,48},{48,64},{64,80},{80,96},{96,112},{112,128},... | collective-permute-start | bytes 393224 | tf_op jit(solution)/shard_map/ppermute | solution.py:15
  158.1 50.3 %all-to-all-start.3 = ((bf16[256,8,1,128]{3,1,2,0:T(8,128)(2,1)}), bf16[256,8,1,128]{3,1,2,0:T(8,128)(2,1)S(1)}, u32[]{:S(2)}, u32[]{:S(2)}) async-start(bf16[256,8,1,128]{3,1,2,0:T(8,128)(2,1)} %bitcast.39), calls=%async_computation.3 | async-start | bytes 1048576 | tf_op jit(solution)/shard_map/all_to_all | solution.py:132
  210.6 4.6 %collective-permute-start.11 = (f32[16,1,16,128]{3,1,0,2:T(1,128)S(1)}, f32[16,1,16,128]{3,1,0,2:T(1,128)S(1)}, u32[]{:S(2)}, u32[]{:S(2)}) collective-permute-start(f32[16,1,16,128]{3,1,0,2:T(1,128)S(1)} %get-tuple-element.32), channel_id=1, source_target_pairs={{16,0},{32,16},{48,32},{64,48},{80,64},{96,80},{112,96},{128,112},... | collective-permute-start | bytes 393224 | tf_op jit(solution)/shard_map/ppermute | solution.py:18
  212.5 7.2 %collective-permute-start.10 = (f32[16,1,16,128]{3,1,0,2:T(1,128)S(1)}, f32[16,1,16,128]{3,1,0,2:T(1,128)S(1)}, u32[]{:S(2)}, u32[]{:S(2)}) collective-permute-start(f32[16,1,16,128]{3,1,0,2:T(1,128)S(1)} %get-tuple-element.33), channel_id=1, source_target_pairs={{0,16},{16,32},{32,48},{48,64},{64,80},{80,96},{96,112},{112,128},... | collective-permute-start | bytes 393224 | tf_op jit(solution)/shard_map/ppermute | solution.py:15
  222.9 4.6 %collective-permute-start.13 = (f32[16,1,16,128]{3,1,0,2:T(1,128)S(1)}, f32[16,1,16,128]{3,1,0,2:T(1,128)S(1)}, u32[]{:S(2)}, u32[]{:S(2)}) collective-permute-start(f32[16,1,16,128]{3,1,0,2:T(1,128)S(1)} %get-tuple-element.30), channel_id=1, source_target_pairs={{16,0},{32,16},{48,32},{64,48},{80,64},{96,80},{112,96},{128,112},... | collective-permute-start | bytes 393224 | tf_op jit(solution)/shard_map/ppermute | solution.py:18
  224.8 7.2 %collective-permute-start.12 = (f32[16,1,16,128]{3,1,0,2:T(1,128)S(1)}, f32[16,1,16,128]{3,1,0,2:T(1,128)S(1)}, u32[]{:S(2)}, u32[]{:S(2)}) collective-permute-start(f32[16,1,16,128]{3,1,0,2:T(1,128)S(1)} %get-tuple-element.31), channel_id=1, source_target_pairs={{0,16},{16,32},{32,48},{48,64},{64,80},{80,96},{96,112},{112,128},... | collective-permute-start | bytes 393224 | tf_op jit(solution)/shard_map/ppermute | solution.py:15
  235.2 4.8 %collective-permute-start.15 = (f32[16,1,16,128]{3,1,0,2:T(1,128)S(1)}, f32[16,1,16,128]{3,1,0,2:T(1,128)S(1)}, u32[]{:S(2)}, u32[]{:S(2)}) collective-permute-start(f32[16,1,16,128]{3,1,0,2:T(1,128)S(1)} %get-tuple-element.28), channel_id=1, source_target_pairs={{16,0},{32,16},{48,32},{64,48},{80,64},{96,80},{112,96},{128,112},... | collective-permute-start | bytes 393224 | tf_op jit(solution)/shard_map/ppermute | solution.py:18
  237.1 7.2 %collective-permute-start.14 = (f32[16,1,16,128]{3,1,0,2:T(1,128)S(1)}, f32[16,1,16,128]{3,1,0,2:T(1,128)S(1)}, u32[]{:S(2)}, u32[]{:S(2)}) collective-permute-start(f32[16,1,16,128]{3,1,0,2:T(1,128)S(1)} %get-tuple-element.29), channel_id=1, source_target_pairs={{0,16},{16,32},{32,48},{48,64},{64,80},{80,96},{96,112},{112,128},... | collective-permute-start | bytes 393224 | tf_op jit(solution)/shard_map/ppermute | solution.py:15
  247.4 4.6 %collective-permute-start.17 = (f32[16,1,16,128]{3,1,0,2:T(1,128)S(1)}, f32[16,1,16,128]{3,1,0,2:T(1,128)S(1)}, u32[]{:S(2)}, u32[]{:S(2)}) collective-permute-start(f32[16,1,16,128]{3,1,0,2:T(1,128)S(1)} %get-tuple-element.26), channel_id=1, source_target_pairs={{16,0},{32,16},{48,32},{64,48},{80,64},{96,80},{112,96},{128,112},... | collective-permute-start | bytes 393224 | tf_op jit(solution)/shard_map/ppermute | solution.py:18
  249.3 7.2 %collective-permute-start.16 = (f32[16,1,16,128]{3,1,0,2:T(1,128)S(1)}, f32[16,1,16,128]{3,1,0,2:T(1,128)S(1)}, u32[]{:S(2)}, u32[]{:S(2)}) collective-permute-start(f32[16,1,16,128]{3,1,0,2:T(1,128)S(1)} %get-tuple-element.27), channel_id=1, source_target_pairs={{0,16},{16,32},{32,48},{48,64},{64,80},{80,96},{96,112},{112,128},... | collective-permute-start | bytes 393224 | tf_op jit(solution)/shard_map/ppermute | solution.py:15
  (10 other events, 137.9 us)
where the time goes:
time: 261 us; the launch traced here: 259 us
  blocking collectives  113 us (43%)
  starting transfers between devices  60 us (23%)
  waiting for transfers between devices  40.9 us (16%)
  other arithmetic  32.4 us (12%)
  local copies, waits for them, and re-layouts  7.72 us (3%)
  matrix products  3.54 us (1%)
    all_gather x2, blocking collectives, body(): lax.all_gather(band_denominator.reshape(slab_depth, band_rows, plane_cols...  93.7 us
    ppermute x9, waiting for transfers between devices, extended(): lax.ppermute(lax.slice_in_dim(block, block.shape[dim] - width, None, axis...  35.2 us
    ppermute x9, starting transfers between devices, extended(): lax.ppermute(lax.slice_in_dim(block, block.shape[dim] - width, None, axis...  21.6 us
    ppermute x9, starting transfers between devices, extended(): lax.ppermute(lax.slice_in_dim(block, 0, width, axis=dim), axis, backward)  19.9 us
    all_to_all x1, blocking collectives, body(): lax.all_to_all(concentration, 'spec', split_axis=2, concat_axis=0, tiled=...  19.7 us
    mul x8, other arithmetic, body(): mobile_padded = extended(mobile_share * field, (('slab', 1),), 1)  12.8 us
    all_to_all x1, starting transfers between devices, body(): lax.all_to_all(concentration, 'spec', split_axis=2, concat_axis=0, tiled=...  11 us
    all_to_all x2, starting transfers between devices, body(): lax.all_to_all(renewed.reshape(species, slab_depth, band_rows, plane_cols...  7.48 us
  transfers between devices with their start and end apart: 21, of which 9 were waited for; matrix products, arithmetic and copies ran while one was open for 5% of the time, Pallas kernels for 0%

commit v1 on v0

v1 whole, which is shorter than its diff:
```python
import functools

import jax
import jax.numpy as jnp
from jax import lax
from jax.experimental import pallas as pl
from jax.experimental.pallas import tpu as pltpu
from jax.sharding import PartitionSpec as P

SUB = 4
STEPS = 2
N = 16
NSLAB = 16
SP = 16
L = 8
E = L + 2 * SUB
Y = 16
X = 128
S = 256
M = 8
MESH = pl.DeviceIdType.MESH
f32 = jnp.float32
bf16 = jnp.bfloat16


def column(row):
    n = row.shape[1]
    eye = lax.broadcasted_iota(jnp.int32, (n, n), 0) == lax.broadcasted_iota(jnp.int32, (n, n), 1)
    return jnp.sum(jnp.where(eye, jnp.broadcast_to(row, (n, n)), 0.0), axis=1, keepdims=True)


def kernel(
    c_ref, inhibit_ref, priming_ref, produce_ref, vectors_ref, capacity_ref, affinity_ref, tort_ref, dif_ref,
    vel_ref, mat_ref, root_ref, out_ref,
    c32, send_a, recv_a, send_b, ren, den_send, den,
    matx, velx, tpad, cxr, cxl, fy, diag, cz, vz, ratio, uptake, mr, hs, ex, aff, root_b,
    fld, share, mob, outs,
    sem_as, sem_ar, sem_bs, sem_br, sem_ds, sem_dr, sem_hs, sem_hr, sem_gs, sem_gr, sem_cs, sem_cr,
):
    me = lax.axis_index("spec")
    slab = lax.axis_index("slab")
    below = lax.rem(slab + 1, NSLAB)
    above = lax.rem(slab + NSLAB - 1, NSLAB)

    barrier = pltpu.get_barrier_semaphore()

    @pl.loop(1, N)
    def _(d):
        pl.semaphore_signal(barrier, inc=1, device_id={"spec": lax.rem(me + d, N)}, device_id_type=MESH)

    for t in (below, above):
        pl.semaphore_signal(barrier, inc=1, device_id={"slab": t}, device_id_type=MESH)

    @pl.loop(0, SP)
    def _(s):
        for l in range(L):
            c32[pl.ds(s * L * Y + l * Y, Y), :] = c_ref[s, l].astype(f32)

    pl.semaphore_wait(barrier, N + 1)

    def copy_a(st, t, src):
        return pltpu.make_async_remote_copy(
            send_a.at[st, t], recv_a.at[st, me], sem_as.at[st, t], sem_ar.at[st, me],
            device_id={"spec": t}, device_id_type=MESH,
        )

    def wait_a(st, src):
        pltpu.make_async_remote_copy(
            send_a.at[st, src], recv_a.at[st, src], sem_as.at[st, src], sem_ar.at[st, src],
            device_id={"spec": src}, device_id_type=MESH,
        ).wait_recv()

    def wait_a_sent(st, t):
        copy_a(st, t, me).wait_send()

    def copy_b(st, t):
        return pltpu.make_async_remote_copy(
            send_b.at[st, t], ren.at[st, me, pl.ds(SUB, L)], sem_bs.at[st, t], sem_br.at[st, me],
            device_id={"spec": t}, device_id_type=MESH,
        )

    def copy_d(st, t):
        return pltpu.make_async_remote_copy(
            den_send.at[st], den.at[st, me, pl.ds(1, 2)], sem_ds.at[st, t], sem_dr.at[st, me],
            device_id={"spec": t}, device_id_type=MESH,
        )

    def wait_b(st, src):
        pltpu.make_async_remote_copy(
            send_b.at[st, src], ren.at[st, src, pl.ds(SUB, L)], sem_bs.at[st, src], sem_br.at[st, src],
            device_id={"spec": src}, device_id_type=MESH,
        ).wait_recv()

    def wait_d(st, src):
        pltpu.make_async_remote_copy(
            den_send.at[st], den.at[st, src, pl.ds(1, 2)], sem_ds.at[st, src], sem_dr.at[st, src],
            device_id={"spec": src}, device_id_type=MESH,
        ).wait_recv()

    def copies_h(st, y):
        down = pltpu.make_async_remote_copy(
            ren.at[st, y, pl.ds(L, SUB)], ren.at[st, y, pl.ds(0, SUB)], sem_hs.at[st, 0, y], sem_hr.at[st, 0, y],
            device_id={"slab": below}, device_id_type=MESH,
        )
        up = pltpu.make_async_remote_copy(
            ren.at[st, y, pl.ds(SUB, SUB)], ren.at[st, y, pl.ds(L + SUB, SUB)], sem_hs.at[st, 1, y], sem_hr.at[st, 1, y],
            device_id={"slab": above}, device_id_type=MESH,
        )
        return down, up

    def copies_g(st):
        down = pltpu.make_async_remote_copy(
            den.at[st, :, 2], den.at[st, :, 0], sem_gs.at[st, 0], sem_gr.at[st, 0],
            device_id={"slab": below}, device_id_type=MESH,
        )
        up = pltpu.make_async_remote_copy(
            den.at[st, :, 1], den.at[st, :, 3], sem_gs.at[st, 1], sem_gr.at[st, 1],
            device_id={"slab": above}, device_id_type=MESH,
        )
        return down, up

    def copies_c():
        out = []
        for i, (ref, dst) in enumerate(((mat_ref, matx), (vel_ref, velx))):
            out.append(pltpu.make_async_remote_copy(
                ref.at[pl.ds(L - SUB, SUB)], dst.at[pl.ds(0, SUB)], sem_cs.at[2 * i], sem_cr.at[2 * i],
                device_id={"slab": below}, device_id_type=MESH,
            ))
            out.append(pltpu.make_async_remote_copy(
                ref.at[pl.ds(0, SUB)], dst.at[pl.ds(L + SUB, SUB)], sem_cs.at[2 * i + 1], sem_cr.at[2 * i + 1],
                device_id={"slab": above}, device_id_type=MESH,
            ))
        return out

    @pl.loop(1, N + 1)
    def _(d):
        t = lax.rem(me + d, N)
        for l in range(L):
            send_a[0, t, l] = c32[pl.ds(l * Y + t, SP, stride=L * Y), :].astype(bf16)

        @pl.when(d < N)
        def _():
            copy_a(0, t, me).start()

    rims = copies_c()
    for cp in rims:
        cp.start()

    for l in range(L):
        matx[SUB + l] = mat_ref[l]
        velx[SUB + l] = vel_ref[l]
    for half in range(2):
        rows = pl.ds(half * 128, 128)
        for i, ref in enumerate((mr, hs, ex)):
            ref[rows, :] = jnp.broadcast_to(column(vectors_ref[2 * i + half : 2 * i + half + 1, :]), (128, X))
        for g in range(M):
            up = capacity_ref[g : g + 1, rows] * affinity_ref[g : g + 1, rows]
            uptake[g, rows, :] = jnp.broadcast_to(column(up), (128, X))
    a_hi = affinity_ref[...].astype(bf16)
    aff[0:M, :] = a_hi.astype(f32)
    aff[M : 2 * M, :] = affinity_ref[...] - a_hi.astype(f32)
    for l in range(L):
        root_b[l : l + 1, :] = root_ref[l, pl.ds(me, 1), :].astype(f32)
    dif = jnp.broadcast_to(column(dif_ref[...]), (SP, X))
    dif_h = (dif[0:8], dif[8:16])
    lane = lax.broadcasted_iota(jnp.int32, (Y, X), 1)
    zero_row = jnp.zeros((SP, X), f32)
    tpad[...] = jnp.zeros_like(tpad)
    for k in range(SUB):
        for e in range(E):
            mob[k, 0, e] = zero_row
            mob[k, Y + 1, e] = zero_row

    for cp in rims:
        cp.wait_recv()

    def inside(e):
        layer = slab * L + e - SUB
        return jnp.where((layer >= 0) & (layer < NSLAB * L), 1.0, 0.0).astype(f32)

    def tort_of(e):
        m = matx[e]
        t = jnp.zeros((Y, X), f32)
        for g in range(M):
            t = jnp.where(m == g, tort_ref[g], t)
        return t * inside(e)

    @pl.loop(0, E)
    def _(e):
        t = tort_of(e)
        tpad[e, pl.ds(8, Y), :] = t

    @pl.loop(0, E)
    def _(e):
        t = tpad[e, pl.ds(8, Y), :]
        right = 0.5 * (t + jnp.where(lane == X - 1, 0.0, pltpu.roll(t, X - 1, 1)))
        left = 0.5 * (t + jnp.where(lane == 0, 0.0, pltpu.roll(t, 1, 1)))
        north = 0.5 * (t + tpad[e, pl.ds(7, Y), :])
        south = 0.5 * (t + tpad[e, pl.ds(9, Y), :])
        total = right + left + north + south
        right = jnp.where(lane == X - 1, 0.0, right)
        left = jnp.where(lane == 0, 0.0, left)
        nxt = tpad[jnp.minimum(e + 1, E - 1), pl.ds(8, Y), :]
        zface = 0.5 * (t + nxt)
        v = velx[e]
        for y in range(Y):
            for ref, val in ((cxr, right), (cxl, left), (diag, total), (cz, zface), (vz, v)):
                ref[y, e] = jnp.broadcast_to(val[y : y + 1], (8, X))
            fy[y, e] = jnp.broadcast_to(north[y : y + 1], (8, X))
        fy[Y, e] = jnp.broadcast_to(south[Y - 1 : Y], (8, X))

    ups = [uptake[g, pl.ds(pl.multiple_of(me * SP, SP), SP), :] for g in range(M)]

    @pl.loop(0, E)
    def _(e):
        m = matx[e]
        for y in range(Y):
            row = jnp.broadcast_to(m[y : y + 1], (SP, X))
            r = ups[0]
            for g in range(1, M):
                r = jnp.where(row == g, ups[g], r)
            ratio[y, e] = r

    def react(st):
        @pl.loop(0, L // 2)
        def _(p):
            def both(a):
                return jnp.concatenate([a, a], axis=1)

            def band(l):
                return recv_a[st, :, l].reshape(S, X)

            l0 = 2 * p
            gathered = jnp.concatenate([band(l0), band(l0 + 1)], axis=1)
            inhibition = jnp.dot(inhibit_ref[...], gathered, preferred_element_type=f32)
            boost = jnp.dot(priming_ref[...], gathered, preferred_element_type=f32)
            dissolved = gathered.astype(f32)
            rate = both(mr[...]) * (1.0 + boost) / (both(hs[...]) + dissolved + inhibition)
            remaining = dissolved * jnp.exp(-rate)
            consumed = (dissolved - remaining).astype(bf16)
            roots = jnp.concatenate([root_b[pl.ds(l0, 1), :], root_b[pl.ds(l0 + 1, 1), :]], axis=1)
            reacted = (
                remaining
                + jnp.dot(produce_ref[...], consumed, preferred_element_type=f32)
                + both(ex[...]) * jnp.broadcast_to(roots, (S, 2 * X))
            )
            renewed = reacted.astype(bf16)
            low = (reacted - renewed.astype(f32)).astype(bf16)
            a16 = aff[...].astype(bf16)
            s_hi = jnp.dot(a16, renewed, preferred_element_type=f32)
            s_lo = jnp.dot(a16, low, preferred_element_type=f32)
            sums = s_hi[0:M] + s_hi[M:] + s_lo[0:M]
            for i in range(2):
                cols = slice(i * X, (i + 1) * X)
                labels = mat_ref[l0 + i, pl.ds(me, 1), :]
                hit = jnp.broadcast_to(labels, (M, X)) == lax.broadcasted_iota(jnp.int32, (M, X), 0)
                d = 1.0 + jnp.sum(jnp.where(hit, sums[:, cols], 0.0), axis=0, keepdims=True)
                den_send[st, p // 2, pl.ds(lax.rem(l0, SUB) + i, 1), :] = d
                send_b[st, :, l0 + i] = renewed[:, cols].reshape(N, SP, X)

    def prep(st, es, rim):
        @pl.loop(0, Y)
        def _(y):
            for e in es:
                r = ren[st, y, e].astype(f32)
                d = jnp.broadcast_to(den[st, y, e // SUB, e % SUB : e % SUB + 1, :], (SP, X))
                s = d / (d + ratio[y, e])
                if rim:
                    s = s * inside(e)
                fld[y, e] = r
                share[y, e] = s
                mob[0, y + 1, e] = s * r

    def substep(k, es, finish=None):
        last = k == SUB - 1

        @pl.loop(1, N + 1)
        def _(j):
            y = lax.rem(me + j, N)
            a = es[0]
            halves = (pl.ds(0, 8), pl.ds(8, 8))
            cen = [mob[k, y + 1, a, h, :] for h in halves]
            prev = [mob[k, y + 1, a - 1, h, :] for h in halves]
            czp, vp = cz[y, a - 1], vz[y, a - 1]
            fzp = [czp * (cen[i] - prev[i]) for i in range(2)]
            wp = [vp * prev[i] for i in range(2)]
            for e in es:
                cze, ve = cz[y, e], vz[y, e]
                xr, xl, n_, s_, dg = cxr[y, e], cxl[y, e], fy[y, e], fy[y + 1, e], diag[y, e]
                done = []
                for i, h in enumerate(halves):
                    m = cen[i]
                    nxt = mob[k, y + 1, e + 1, h, :]
                    fz = cze * (nxt - m)
                    w = ve * m
                    acc = fz - fzp[i]
                    acc += xr * pltpu.roll(m, X - 1, 1) + xl * pltpu.roll(m, 1, 1)
                    acc += n_ * mob[k, y, e, h, :] + s_ * mob[k, y + 2, e, h, :]
                    acc -= dg * m
                    f = fld[y, e, h, :] + (wp[i] - w) + dif_h[i] * acc
                    if last:
                        done.append(f)
                    else:
                        fld[y, e, h, :] = f
                        mob[k + 1, y + 1, e, h, :] = share[y, e, h, :] * f
                    cen[i], fzp[i], wp[i] = nxt, fz, w
                if last:
                    finish(y, e - SUB, jnp.concatenate(done, axis=0))
            if last:
                finish(y, None, j)

    for st in range(STEPS):
        recv_a[st, me] = send_a[st, me]

        @pl.loop(1, N)
        def _(d):
            wait_a(st, lax.rem(me + N - d, N))

        react(st)

        @pl.loop(1, N)
        def _(d):
            t = lax.rem(me + d, N)
            copy_d(st, t).start()
            copy_b(st, t).start()

        ren[st, me, pl.ds(SUB, L)] = send_b[st, me]
        den[st, me, pl.ds(1, 2)] = den_send[st]
        for cp in copies_h(st, me):
            cp.start()

        @pl.loop(1, N)
        def _(d):
            src = lax.rem(me + N - d, N)
            wait_d(st, src)
            wait_b(st, src)
            for cp in copies_h(st, src):
                cp.start()

        for cp in copies_g(st):
            cp.start()
        prep(st, range(SUB, SUB + L), False)
        for k in range(SUB - 1):
            substep(k, range(SUB + 1 + k, SUB + L - 1 - k))

        for cp in copies_g(st):
            cp.wait_recv()

        @pl.loop(0, Y)
        def _(y):
            for cp in copies_h(st, y):
                cp.wait_recv()

        prep(st, [*range(0, SUB), *range(SUB + L, E)], True)
        for k in range(SUB - 1):
            substep(k, range(k + 1, SUB + 1 + k))
            substep(k, range(SUB + L - 1 - k, E - 1 - k))
        if st < STEPS - 1:

            def finish(y, l, f):
                if l is not None:
                    send_a[st + 1, y, l] = f.astype(bf16)
                else:

                    @pl.when(f < N)
                    def _():
                        copy_a(st + 1, y, me).start()

        else:

            def finish(y, l, f):
                if l is not None:
                    outs[pl.ds(pl.multiple_of(l * Y * SP + y * SP, SP), SP), :] = f

        substep(SUB - 1, range(SUB, SUB + L), finish)

    @pl.loop(0, SP)
    def _(s):
        for l in range(L):
            out_ref[s, l] = outs[pl.ds(l * Y * SP + s, Y, stride=SP), :].astype(bf16)

    for cp in rims:
        cp.wait_send()
    for st in range(STEPS):

        @pl.loop(1, N)
        def _(d):
            t = lax.rem(me + d, N)
            wait_a_sent(st, t)
            copy_d(st, t).wait_send()
            copy_b(st, t).wait_send()

        @pl.loop(0, Y)
        def _(y):
            for cp in copies_h(st, y):
                cp.wait_send()

        for cp in copies_g(st):
            cp.wait_send()


def body(
    concentration, inhibit, priming, produce, max_rate, half_saturation, exudate,
    sorption_capacity, sorption_affinity, tortuosity, diffusivity, velocity, material, root_mask,
):
    vectors = jnp.stack([max_rate, half_saturation, exudate]).reshape(6, 128)
    vmem = pl.BlockSpec(memory_space=pltpu.VMEM)
    dma = pltpu.SemaphoreType.DMA
    big = (Y, E, SP, X)
    rep = (Y, E, 8, X)
    return pl.pallas_call(
        kernel,
        out_shape=jax.ShapeDtypeStruct((SP, L, Y, X), bf16),
        in_specs=[vmem] * 7 + [pl.BlockSpec(memory_space=pltpu.SMEM)] + [vmem] * 4,
        out_specs=vmem,
        scratch_shapes=[
            pltpu.VMEM((SP * L * Y, X), f32),
            pltpu.VMEM((STEPS, N, L, SP, X), bf16),
            pltpu.VMEM((STEPS, N, L, SP, X), bf16),
            pltpu.VMEM((STEPS, N, L, SP, X), bf16),
            pltpu.VMEM((STEPS, Y, E, SP, X), bf16),
            pltpu.VMEM((STEPS, 2, SUB, X), f32),
            pltpu.VMEM((STEPS, Y, 4, SUB, X), f32),
            pltpu.VMEM((E, Y, X), jnp.int32),
            pltpu.VMEM((E, Y, X), f32),
            pltpu.VMEM((E, 32, X), f32),
            pltpu.VMEM(rep, f32),
            pltpu.VMEM(rep, f32),
            pltpu.VMEM((Y + 1, E, 8, X), f32),
            pltpu.VMEM(rep, f32),
            pltpu.VMEM(rep, f32),
            pltpu.VMEM(rep, f32),
            pltpu.VMEM(big, f32),
            pltpu.VMEM((M, S, X), f32),
            pltpu.VMEM((S, X), f32),
            pltpu.VMEM((S, X), f32),
            pltpu.VMEM((S, X), f32),
            pltpu.VMEM((2 * M, S), f32),
            pltpu.VMEM((L, X), f32),
            pltpu.VMEM(big, f32),
            pltpu.VMEM(big, f32),
            pltpu.VMEM((SUB, Y + 2, E, SP, X), f32),
            pltpu.VMEM((L * Y * SP, X), f32),
            dma((STEPS, N)), dma((STEPS, N)),
            dma((STEPS, N)), dma((STEPS, N)),
            dma((STEPS, N)), dma((STEPS, N)),
            dma((STEPS, 2, Y)), dma((STEPS, 2, Y)),
            dma((STEPS, 2)), dma((STEPS, 2)),
            dma((4,)), dma((4,)),
        ],
        compiler_params=pltpu.CompilerParams(
            collective_id=0, has_side_effects=True, vmem_limit_bytes=48 * 2**20
        ),
    )(
        concentration, inhibit, priming, produce, vectors, sorption_capacity, sorption_affinity, tortuosity,
        diffusivity.reshape(1, SP), velocity, material, root_mask,
    )


def solution(mesh):
    in_specs = (
        P("spec", "slab", None, None),
        P(), P(), P(), P(), P(), P(), P(), P(), P(),
        P("spec"),
        P("slab", None, None),
        P("slab", None, None),
        P("slab", None, None),
    )
    out_specs = P("spec", "slab", None, None)
    return jax.shard_map(body, mesh=mesh, in_specs=in_specs, out_specs=out_specs, check_vma=False)
```

time: 261 us -> 124 us (0.48)
  Pallas kernels: 0 us -> 114 us
  blocking collectives: 113 us -> 0 us
  starting transfers between devices: 60 us -> 0 us
  waiting for transfers between devices: 40.9 us -> 0 us
  other arithmetic: 32.4 us -> 0.01 us
  matrix products: 3.54 us -> 0 us
    pallas_call x0 -> x1, Pallas kernels: none -> 114 us  [body(): pl.pallas_call(kernel, out_shape=jax.ShapeDtypeStruct((SP, L, Y, X), bf16...]
    all_gather x2 -> x0, blocking collectives: 93.7 us -> none  [body(): lax.all_gather(band_denominator.reshape(slab_depth, band_rows, plane_cols...]
    ppermute x18 -> x0, starting transfers between devices: 41.5 us -> none  [the longest x9 21.6 us: extended(): lax.ppermute(lax.slice_in_dim(block, block.shape[dim] - width, None, axis...]
    ppermute x18 -> x0, waiting for transfers between devices: 35.2 us -> none  [the longest x9 35.2 us: extended(): lax.ppermute(lax.slice_in_dim(block, block.shape[dim] - width, None, axis...]
    mul x28 -> x0, other arithmetic: 19.8 us -> none  [the longest x8 12.8 us: body(): mobile_padded = extended(mobile_share * field, (('slab', 1),), 1)]
    all_to_all x1 -> x0, blocking collectives: 19.7 us -> none  [body(): lax.all_to_all(concentration, 'spec', split_axis=2, concat_axis=0, tiled=...]
    all_to_all x3 -> x0, starting transfers between devices: 18.5 us -> none  [the longest x1 11 us: body(): lax.all_to_all(concentration, 'spec', split_axis=2, concat_axis=0, tiled=...]
    all_to_all x3 -> x0, waiting for transfers between devices: 5.73 us -> none  [the longest x1 5.73 us: body(): lax.all_to_all(concentration, 'spec', split_axis=2, concat_axis=0, tiled=...]
  transfers between devices with their start and end apart: 21 -> 0, of which waited for: 9 -> 0; matrix products, arithmetic and copies ran while one was open for 5% -> 0% of each run, Pallas kernels for 0% -> 0%
where the time goes in v1:
time: 124 us; the launch traced here: 122 us
  Pallas kernels  114 us (92%)
  local copies, waits for them, and re-layouts  8.39 us (7%)
    pallas_call x1, Pallas kernels, body(): pl.pallas_call(kernel, out_shape=jax.ShapeDtypeStruct((SP, L, Y, X), bf16...  114 us
    unnamed x29, local copies, waits for them, and re-layouts  8.38 us

profile of v1, /device:TPU:16, one launch (start us, length us, event | category | flops | bytes accessed | tf_op | source)
XLA Modules:
  0.0 122.4 jit_solution(11385332264249961647)
XLA Ops:
  0.0 0.0 copy-start.12
  0.0 0.0 copy-start.13
  0.0 0.0 copy-start.11
  0.0 0.0 copy-start.10
  0.0 0.0 copy-start.7
  0.0 0.0 copy-start.8
  0.0 0.6 copy-done.12
  0.7 0.0 copy-done.13
  0.7 0.0 copy-done.11
  0.7 0.0 copy-start.9
  0.7 0.0 copy-done.10
  0.7 0.0 copy-done.7
  0.8 0.0 copy-done.8
  0.8 0.6 copy-done.9
  1.4 0.0 copy-start
  1.4 1.0 copy-done
  2.4 0.9 copy-done.1
  3.3 0.9 copy-done.2
  4.2 0.9 copy-done.3
  5.1 0.8 copy-done.4
  6.0 0.8 copy-done.5
  6.8 0.8 copy-done.6
  7.7 114.0 %shard_map.136 = bf16[16,8,16,128]{3,2,1,0:T(8,128)(2,1)S(1)} custom-call(bf16[16,8,16,128]{3,2,1,0:T(8,128)(2,1)S(1)} %copy-done, bf16[256,256]{1,0:T(8,128)(2,1)S(1)} %copy-done.1, bf16[256,256]{1,0:T(8,128)(2,1)S(1)} %copy-done.2, bf16[256,256]{1,0:T(8,128)(2,1)S(1)} %copy-done.3, f32[6,128]{1,0:T(8,128)S(1)} %reshape.6.vectors_ref, ...), custom_call_target="tpu_custom_call" | custom-call | tf_op jit(solution)/shard_map/pallas_call | solution.py:411
  121.6 0.8 copy.16
  (8 shorter events, 0.0 us)
Async XLA Ops:
  0.0 0.7 copy-start.12
  0.0 0.7 copy-start.13
  0.0 0.7 copy-start.11
  0.0 0.7 copy-start.10
  0.0 0.7 copy-start.7
  0.0 0.7 copy-start.8
  0.7 0.7 copy-start.9
  1.4 1.0 copy-start
  2.4 0.9 copy-start.1
  3.3 0.9 copy-start.2
  4.2 0.9 copy-start.3
  5.1 0.8 copy-start.4
  6.0 0.8 copy-start.5
  6.8 0.8 copy-start.6

commit v2 on v1

v2 whole, which is shorter than its diff:
```python
import functools

import jax
import jax.numpy as jnp
from jax import lax
from jax.experimental import pallas as pl
from jax.experimental.pallas import tpu as pltpu
from jax.sharding import PartitionSpec as P

SUB = 4
STEPS = 2
N = 16
NSLAB = 16
SP = 16
L = 8
E = L + 2 * SUB
Y = 16
X = 128
S = 256
M = 8
MESH = pl.DeviceIdType.MESH
f32 = jnp.float32
bf16 = jnp.bfloat16


def column(row):
    n = row.shape[1]
    eye = lax.broadcasted_iota(jnp.int32, (n, n), 0) == lax.broadcasted_iota(jnp.int32, (n, n), 1)
    return jnp.sum(jnp.where(eye, jnp.broadcast_to(row, (n, n)), 0.0), axis=1, keepdims=True)


def kernel(
    c_hbm, inhibit_hbm, priming_hbm, produce_hbm, rate_hbm, half_hbm, exudate_hbm, capacity_hbm, affinity_hbm,
    tort_hbm, dif_hbm, vel_hbm, mat_hbm, root_hbm, out_ref,
    c_ref, inhibit_ref, priming_ref, produce_ref, rate_ref, half_ref, exudate_ref, capacity_ref, affinity_ref,
    tort_ref, dif_ref, root_ref, sem_in,
    c32, send_a, recv_a, send_b, ren, den_send, den,
    matx, velx, tpad, cxr, cxl, fy, diag, cz, vz, ratio, uptake, mr, hs, ex, aff, root_b,
    fld, share, mob0, mob1, mob2, mob3, outs,
    sem_as, sem_ar, sem_bs, sem_br, sem_ds, sem_dr, sem_hs, sem_hr, sem_gs, sem_gr, sem_cs, sem_cr,
):
    mob = (mob0, mob1, mob2, mob3)
    me = lax.axis_index("spec")
    slab = lax.axis_index("slab")
    below = lax.rem(slab + 1, NSLAB)
    above = lax.rem(slab + NSLAB - 1, NSLAB)

    own = pl.ds(SUB, L)
    loads = [
        pltpu.make_async_copy(src, dst, sem_in.at[i])
        for i, (src, dst) in enumerate((
            (c_hbm, c_ref), (mat_hbm, matx.at[own]), (vel_hbm, velx.at[own]), (tort_hbm, tort_ref),
            (capacity_hbm, capacity_ref), (affinity_hbm, affinity_ref), (rate_hbm, rate_ref), (half_hbm, half_ref),
            (exudate_hbm, exudate_ref), (dif_hbm, dif_ref), (root_hbm, root_ref), (inhibit_hbm, inhibit_ref),
            (priming_hbm, priming_ref), (produce_hbm, produce_ref),
        ))
    ]
    for cp in loads:
        cp.start()

    barrier = pltpu.get_barrier_semaphore()

    @pl.loop(1, N)
    def _(d):
        pl.semaphore_signal(barrier, inc=1, device_id={"spec": lax.rem(me + d, N)}, device_id_type=MESH)

    for t in (below, above):
        pl.semaphore_signal(barrier, inc=1, device_id={"slab": t}, device_id_type=MESH)

    loads[0].wait()

    @pl.loop(0, SP)
    def _(s):
        for l in range(L):
            c32[pl.ds(s * L * Y + l * Y, Y), :] = c_ref[s, l].astype(f32)

    pl.semaphore_wait(barrier, N + 1)

    def half(q):
        return pl.ds(q * SUB, SUB)

    def copy_a(st, q, t, slot):
        return pltpu.make_async_remote_copy(
            send_a.at[st, t, half(q)], recv_a.at[st, slot, half(q)], sem_as.at[st, q, t], sem_ar.at[st, q, slot],
            device_id={"spec": t}, device_id_type=MESH,
        )

    def copy_b(st, q, t, slot):
        return pltpu.make_async_remote_copy(
            send_b.at[st, t, half(q)], ren.at[st, slot, pl.ds(SUB + q * SUB, SUB)], sem_bs.at[st, q, t],
            sem_br.at[st, q, slot], device_id={"spec": t}, device_id_type=MESH,
        )

    def copy_d(st, q, t, slot):
        return pltpu.make_async_remote_copy(
            den_send.at[st, q], den.at[st, slot, 1 + q], sem_ds.at[st, q, t], sem_dr.at[st, q, slot],
            device_id={"spec": t}, device_id_type=MESH,
        )

    def copy_h(st, q, y):
        return pltpu.make_async_remote_copy(
            ren.at[st, y, pl.ds(SUB + q * SUB, SUB)], ren.at[st, y, pl.ds((1 - q) * (SUB + L), SUB)],
            sem_hs.at[st, q, y], sem_hr.at[st, q, y],
            device_id={"slab": below if q else above}, device_id_type=MESH,
        )

    def copy_g(st, q):
        return pltpu.make_async_remote_copy(
            den.at[st, :, 1 + q], den.at[st, :, 3 * (1 - q)], sem_gs.at[st, q], sem_gr.at[st, q],
            device_id={"slab": below if q else above}, device_id_type=MESH,
        )

    def copies_c():
        out = []
        for i, ref in enumerate((matx, velx)):
            out.append(pltpu.make_async_remote_copy(
                ref.at[pl.ds(L, SUB)], ref.at[pl.ds(0, SUB)], sem_cs.at[2 * i], sem_cr.at[2 * i],
                device_id={"slab": below}, device_id_type=MESH,
            ))
            out.append(pltpu.make_async_remote_copy(
                ref.at[pl.ds(SUB, SUB)], ref.at[pl.ds(L + SUB, SUB)], sem_cs.at[2 * i + 1], sem_cr.at[2 * i + 1],
                device_id={"slab": above}, device_id_type=MESH,
            ))
        return out

    for q in range(2):

        @pl.loop(1, N + 1)
        def _(d):
            t = lax.rem(me + d, N)
            for l in range(q * SUB, q * SUB + SUB):
                send_a[0, t, l] = c32[pl.ds(l * Y + t, SP, stride=L * Y), :].astype(bf16)

            @pl.when(d < N)
            def _():
                copy_a(0, q, t, me).start()

    for cp in loads[1:]:
        cp.wait()
    rims = copies_c()
    for cp in rims:
        cp.start()

    for i in range(2):
        rows = pl.ds(i * 128, 128)
        for ref, src in ((mr, rate_ref), (hs, half_ref), (ex, exudate_ref)):
            ref[rows, :] = jnp.broadcast_to(column(src[:, rows]), (128, X))
        for g in range(M):
            up = capacity_ref[g : g + 1, rows] * affinity_ref[g : g + 1, rows]
            uptake[g, rows, :] = jnp.broadcast_to(column(up), (128, X))
    a_hi = affinity_ref[...].astype(bf16)
    aff[0:M, :] = a_hi.astype(f32)
    aff[M : 2 * M, :] = affinity_ref[...] - a_hi.astype(f32)
    for l in range(L):
        root_b[l : l + 1, :] = root_ref[l, pl.ds(me, 1), :].astype(f32)
    dif = jnp.broadcast_to(column(dif_ref[...]), (SP, X))
    dif_h = (dif[0:8], dif[8:16])
    lane = lax.broadcasted_iota(jnp.int32, (Y, X), 1)
    zero_row = jnp.zeros((SP, X), f32)
    tpad[...] = jnp.zeros_like(tpad)
    for k in range(SUB):
        for e in range(E):
            mob[k][0, e] = zero_row
            mob[k][Y + 1, e] = zero_row

    for cp in rims:
        cp.wait_recv()

    def inside(e):
        layer = slab * L + e - SUB
        return jnp.where((layer >= 0) & (layer < NSLAB * L), 1.0, 0.0).astype(f32)

    torts = [jnp.broadcast_to(tort_ref[:, g : g + 1], (Y, X)) for g in range(M)]

    def tort_of(e):
        m = matx[e]
        t = jnp.zeros((Y, X), f32)
        for g in range(M):
            t = jnp.where(m == g, torts[g], t)
        return t * inside(e)

    @pl.loop(0, E)
    def _(e):
        t = tort_of(e)
        tpad[e, pl.ds(8, Y), :] = t

    @pl.loop(0, E)
    def _(e):
        t = tpad[e, pl.ds(8, Y), :]
        right = 0.5 * (t + jnp.where(lane == X - 1, 0.0, pltpu.roll(t, X - 1, 1)))
        left = 0.5 * (t + jnp.where(lane == 0, 0.0, pltpu.roll(t, 1, 1)))
        north = 0.5 * (t + tpad[e, pl.ds(7, Y), :])
        south = 0.5 * (t + tpad[e, pl.ds(9, Y), :])
        total = right + left + north + south
        right = jnp.where(lane == X - 1, 0.0, right)
        left = jnp.where(lane == 0, 0.0, left)
        nxt = tpad[jnp.minimum(e + 1, E - 1), pl.ds(8, Y), :]
        zface = 0.5 * (t + nxt)
        v = velx[e]
        for y in range(Y):
            for ref, val in ((cxr, right), (cxl, left), (diag, total), (cz, zface), (vz, v)):
                ref[y, e] = jnp.broadcast_to(val[y : y + 1], (8, X))
            fy[y, e] = jnp.broadcast_to(north[y : y + 1], (8, X))
        fy[Y, e] = jnp.broadcast_to(south[Y - 1 : Y], (8, X))

    ups = [uptake[g, pl.ds(pl.multiple_of(me * SP, SP), SP), :] for g in range(M)]

    @pl.loop(0, E)
    def _(e):
        m = matx[e]
        for y in range(Y):
            row = jnp.broadcast_to(m[y : y + 1], (SP, X))
            r = ups[0]
            for g in range(1, M):
                r = jnp.where(row == g, ups[g], r)
            ratio[y, e] = r

    def react(st, q):
        @pl.loop(q * SUB // 2, (q + 1) * SUB // 2)
        def _(p):
            def both(a):
                return jnp.concatenate([a, a], axis=1)

            def band(l):
                return recv_a[st, :, l].reshape(S, X)

            l0 = 2 * p
            gathered = jnp.concatenate([band(l0), band(l0 + 1)], axis=1)
            inhibition = jnp.dot(inhibit_ref[...], gathered, preferred_element_type=f32)
            boost = jnp.dot(priming_ref[...], gathered, preferred_element_type=f32)
            dissolved = gathered.astype(f32)
            rate = both(mr[...]) * (1.0 + boost) / (both(hs[...]) + dissolved + inhibition)
            remaining = dissolved * jnp.exp(-rate)
            consumed = (dissolved - remaining).astype(bf16)
            roots = jnp.concatenate([root_b[pl.ds(l0, 1), :], root_b[pl.ds(l0 + 1, 1), :]], axis=1)
            reacted = (
                remaining
                + jnp.dot(produce_ref[...], consumed, preferred_element_type=f32)
                + both(ex[...]) * jnp.broadcast_to(roots, (S, 2 * X))
            )
            renewed = reacted.astype(bf16)
            low = (reacted - renewed.astype(f32)).astype(bf16)
            a16 = aff[...].astype(bf16)
            s_hi = jnp.dot(a16, renewed, preferred_element_type=f32)
            s_lo = jnp.dot(a16, low, preferred_element_type=f32)
            sums = s_hi[0:M] + s_hi[M:] + s_lo[0:M]
            for i in range(2):
                cols = slice(i * X, (i + 1) * X)
                labels = matx[SUB + l0 + i, pl.ds(me, 1), :]
                hit = jnp.broadcast_to(labels, (M, X)) == lax.broadcasted_iota(jnp.int32, (M, X), 0)
                d = 1.0 + jnp.sum(jnp.where(hit, sums[:, cols], 0.0), axis=0, keepdims=True)
                den_send[st, q, pl.ds(l0 - q * SUB + i, 1), :] = d
                send_b[st, :, l0 + i] = renewed[:, cols].reshape(N, SP, X)

    def prep(st, es, rim):
        @pl.loop(0, Y)
        def _(y):
            vals = []
            for e in es:
                r = ren[st, y, e].astype(f32)
                d = jnp.broadcast_to(den[st, y, e // SUB, e % SUB : e % SUB + 1, :], (SP, X))
                s = d / (d + ratio[y, e])
                if rim:
                    s = s * inside(e)
                vals.append((r, s))
            for e, (r, s) in zip(es, vals):
                fld[y, e] = r
                share[y, e] = s
                mob[0][y + 1, e] = s * r

    def substep(k, spans, rows, finish=None):
        last = k == SUB - 1
        halves = (pl.ds(0, 8), pl.ds(8, 8))

        def span(y, es):
            a = es[0]
            cen = [mob[k][y + 1, a, h, :] for h in halves]
            prev = [mob[k][y + 1, a - 1, h, :] for h in halves]
            czp, vp = cz[y, a - 1], vz[y, a - 1]
            fzp = [czp * (cen[i] - prev[i]) for i in range(2)]
            wp = [vp * prev[i] for i in range(2)]
            done = []
            for e in es:
                cze, ve = cz[y, e], vz[y, e]
                xr, xl, n_, s_, dg = cxr[y, e], cxl[y, e], fy[y, e], fy[y + 1, e], diag[y, e]
                for i, h in enumerate(halves):
                    m = cen[i]
                    nxt = mob[k][y + 1, e + 1, h, :]
                    fz = cze * (nxt - m)
                    w = ve * m
                    acc = fz - fzp[i]
                    acc += xr * pltpu.roll(m, X - 1, 1) + xl * pltpu.roll(m, 1, 1)
                    acc += n_ * mob[k][y, e, h, :] + s_ * mob[k][y + 2, e, h, :]
                    acc -= dg * m
                    done.append(fld[y, e, h, :] + (wp[i] - w) + dif_h[i] * acc)
                    cen[i], fzp[i], wp[i] = nxt, fz, w
            if last:
                for i, e in enumerate(es):
                    finish(y, e - SUB, jnp.concatenate(done[2 * i : 2 * i + 2], axis=0))
            else:
                out = [share[y, e, h, :] for e in es for h in halves]
                out = [a * b for a, b in zip(out, done)]
                for i, e in enumerate(es):
                    for n, h in enumerate(halves):
                        fld[y, e, h, :] = done[2 * i + n]
                        mob[k + 1][y + 1, e, h, :] = out[2 * i + n]

        @pl.loop(0, Y // rows)
        def _(j):
            ys = [lax.rem(me + j * rows + 1 + i, N) for i in range(rows)]
            for y in ys:
                for es in spans:
                    span(y, es)
            if last:
                for i, y in enumerate(ys):
                    finish(y, None, j * rows + 1 + i)

    for st in range(STEPS):
        recv_a[st, me] = send_a[st, me]
        for q in range(2):

            @pl.loop(1, N)
            def _(d):
                src = lax.rem(me + N - d, N)
                copy_a(st, q, src, src).wait_recv()

            react(st, q)

            @pl.loop(1, N)
            def _(d):
                t = lax.rem(me + d, N)
                copy_d(st, q, t, me).start()
                copy_b(st, q, t, me).start()

            ren[st, me, pl.ds(SUB + q * SUB, SUB)] = send_b[st, me, half(q)]
            den[st, me, 1 + q] = den_send[st, q]
            copy_h(st, q, me).start()

        for q in range(2):

            @pl.loop(1, N)
            def _(d):
                src = lax.rem(me + N - d, N)
                copy_d(st, q, src, src).wait_recv()
                copy_b(st, q, src, src).wait_recv()
                copy_h(st, q, src).start()

            copy_g(st, q).start()

        prep(st, range(SUB, SUB + L), False)
        for k in range(SUB - 1):
            substep(k, [range(SUB + 1 + k, SUB + L - 1 - k)], (4, 8, 16)[k])

        for q in range(2):
            copy_g(st, q).wait_recv()

            @pl.loop(0, Y)
            def _(y):
                copy_h(st, q, y).wait_recv()

        prep(st, [*range(0, SUB), *range(SUB + L, E)], True)
        for k in range(SUB - 1):
            substep(k, [range(k + 1, SUB + 1 + k), range(SUB + L - 1 - k, E - 1 - k)], 4)
        for q in range(2):
            if st < STEPS - 1:

                def finish(y, l, f):
                    if l is not None:
                        send_a[st + 1, y, l] = f.astype(bf16)
                    else:

                        @pl.when(f < N)
                        def _():
                            copy_a(st + 1, q, y, me).start()

            else:

                def finish(y, l, f):
                    if l is not None:
                        outs[pl.ds(pl.multiple_of(l * Y * SP + y * SP, SP), SP), :] = f

            substep(SUB - 1, [range(SUB + q * SUB, SUB + (q + 1) * SUB)], 8, finish)

    @pl.loop(0, SP)
    def _(s):
        for l in range(L):
            out_ref[s, l] = outs[pl.ds(l * Y * SP + s, Y, stride=SP), :].astype(bf16)

    for cp in rims:
        cp.wait_send()
    for st in range(STEPS):
        for q in range(2):

            @pl.loop(1, N)
            def _(d):
                t = lax.rem(me + d, N)
                copy_a(st, q, t, me).wait_send()
                copy_d(st, q, t, me).wait_send()
                copy_b(st, q, t, me).wait_send()

            @pl.loop(0, Y)
            def _(y):
                copy_h(st, q, y).wait_send()

            copy_g(st, q).wait_send()


def body(
    concentration, inhibit, priming, produce, max_rate, half_saturation, exudate,
    sorption_capacity, sorption_affinity, tortuosity, diffusivity, velocity, material, root_mask,
):
    vmem = pl.BlockSpec(memory_space=pltpu.VMEM)
    dma = pltpu.SemaphoreType.DMA
    big = (Y, E, SP, X)
    rep = (Y, E, 8, X)
    return pl.pallas_call(
        kernel,
        out_shape=jax.ShapeDtypeStruct((SP, L, Y, X), bf16),
        in_specs=[pl.BlockSpec(memory_space=pltpu.HBM)] * 14,
        out_specs=vmem,
        scratch_shapes=[
            pltpu.VMEM((SP, L, Y, X), bf16),
            pltpu.VMEM((S, S), bf16), pltpu.VMEM((S, S), bf16), pltpu.VMEM((S, S), bf16),
            pltpu.VMEM((1, S), f32), pltpu.VMEM((1, S), f32), pltpu.VMEM((1, S), f32),
            pltpu.VMEM((M, S), f32), pltpu.VMEM((M, S), f32),
            pltpu.VMEM((1, M), f32), pltpu.VMEM((1, SP), f32),
            pltpu.VMEM((L, Y, X), jnp.int32),
            dma((14,)),
            pltpu.VMEM((SP * L * Y, X), f32),
            pltpu.VMEM((STEPS, N, L, SP, X), bf16),
            pltpu.VMEM((STEPS, N, L, SP, X), bf16),
            pltpu.VMEM((STEPS, N, L, SP, X), bf16),
            pltpu.VMEM((STEPS, Y, E, SP, X), bf16),
            pltpu.VMEM((STEPS, 2, SUB, X), f32),
            pltpu.VMEM((STEPS, Y, 4, SUB, X), f32),
            pltpu.VMEM((E, Y, X), jnp.int32),
            pltpu.VMEM((E, Y, X), f32),
            pltpu.VMEM((E, 32, X), f32),
            pltpu.VMEM(rep, f32),
            pltpu.VMEM(rep, f32),
            pltpu.VMEM((Y + 1, E, 8, X), f32),
            pltpu.VMEM(rep, f32),
            pltpu.VMEM(rep, f32),
            pltpu.VMEM(rep, f32),
            pltpu.VMEM(big, f32),
            pltpu.VMEM((M, S, X), f32),
            pltpu.VMEM((S, X), f32),
            pltpu.VMEM((S, X), f32),
            pltpu.VMEM((S, X), f32),
            pltpu.VMEM((2 * M, S), f32),
            pltpu.VMEM((L, X), f32),
            pltpu.VMEM(big, f32),
            pltpu.VMEM(big, f32),
            *[pltpu.VMEM((Y + 2, E, SP, X), f32)] * SUB,
            pltpu.VMEM((L * Y * SP, X), f32),
            dma((STEPS, 2, N)), dma((STEPS, 2, N)),
            dma((STEPS, 2, N)), dma((STEPS, 2, N)),
            dma((STEPS, 2, N)), dma((STEPS, 2, N)),
            dma((STEPS, 2, Y)), dma((STEPS, 2, Y)),
            dma((STEPS, 2)), dma((STEPS, 2)),
            dma((4,)), dma((4,)),
        ],
        compiler_params=pltpu.CompilerParams(
            collective_id=0, has_side_effects=True, vmem_limit_bytes=64 * 2**20 - 65536
        ),
    )(
        concentration, inhibit, priming, produce, max_rate.reshape(1, S), half_saturation.reshape(1, S),
        exudate.reshape(1, S), sorption_capacity, sorption_affinity, tortuosity.reshape(1, M),
        diffusivity.reshape(1, SP), velocity, material, root_mask,
    )


def solution(mesh):
    in_specs = (
        P("spec", "slab", None, None),
        P(), P(), P(), P(), P(), P(), P(), P(), P(),
        P("spec"),
        P("slab", None, None),
        P("slab", None, None),
        P("slab", None, None),
    )
    out_specs = P("spec", "slab", None, None)
    return jax.shard_map(body, mesh=mesh, in_specs=in_specs, out_specs=out_specs, check_vma=False)
```

time: 124 us -> 103 us (0.83); the launches traced: 122 us -> 103 us
  Pallas kernels: 114 us -> 101 us
  local copies, waits for them, and re-layouts: 8.39 us -> 1.89 us
    pallas_call x1, Pallas kernels: 114 us -> 101 us  [body(): pl.pallas_call(kernel, out_shape=jax.ShapeDtypeStruct((SP, L, Y, X), bf16...]
    unnamed x29 -> x1, local copies, waits for them, and re-layouts: 8.38 us -> 1.89 us
where the time goes in v2:
time: 103 us
  Pallas kernels  101 us (98%)
  local copies, waits for them, and re-layouts  1.89 us (2%)
    pallas_call x1, Pallas kernels, body(): pl.pallas_call(kernel, out_shape=jax.ShapeDtypeStruct((SP, L, Y, X), bf16...  101 us

profile of v2, /device:TPU:16, one launch (start us, length us, event | category | flops | bytes accessed | tf_op | source)
XLA Modules:
  0.0 102.7 jit_solution(2957347714382541239)
XLA Ops:
  0.0 100.8 %shard_map.136 = bf16[16,8,16,128]{3,2,1,0:T(8,128)(2,1)} custom-call(bf16[16,8,16,128]{3,2,1,0:T(8,128)(2,1)} %c_hbm.1, bf16[256,256]{1,0:T(8,128)(2,1)} %inhibit_hbm.1, bf16[256,256]{1,0:T(8,128)(2,1)} %priming_hbm.1, bf16[256,256]{1,0:T(8,128)(2,1)} %produce_hbm.1, f32[1,256]{1,0:T(1,128)} %bitcast.5, f32[1,256]{1,0:T(1,128)} %bitcast.6, ...), custom_call_target="tpu_custom_call" | custom-call | tf_op jit(solution)/shard_map/pallas_call | solution.py:416
  100.8 1.9 %copy.16 = bf16[16,8,16,128]{3,2,1,0:T(8,128)(2,1)} copy(bf16[16,8,16,128]{3,2,1,0:T(8,128)(2,1)} %shard_map.136) | data formatting | bytes 1048576

commit v3 on v2

--- a/solution.py
+++ b/solution.py
@@ -58,6 +58,14 @@
     for cp in loads:
         cp.start()
 
+    x, z = me // 4, lax.rem(me, 4)
+
+    def at(dx, dz):
+        return lax.rem(x + dx, 4) * 4 + lax.rem(z + dz, 4)
+
+    far = (2, 1, 3, 0)
+    partners = [at(dx, dz) for dx in far for dz in far if dx or dz]
+
     barrier = pltpu.get_barrier_semaphore()
 
     @pl.loop(1, N)
@@ -74,33 +82,55 @@
         for l in range(L):
             c32[pl.ds(s * L * Y + l * Y, Y), :] = c_ref[s, l].astype(f32)
 
+    @pl.loop(0, N)
+    def _(t):
+        for p in range(L // 2):
+            v = [c32[pl.ds(l * Y + t, SP, stride=L * Y), :] for l in (2 * p, 2 * p + 1)]
+            for h in range(2):
+                pair = jnp.concatenate([v[0][8 * h : 8 * h + 8], v[1][8 * h : 8 * h + 8]], axis=0)
+                send_a[0, t, h, p] = pair.astype(bf16)
+
     pl.semaphore_wait(barrier, N + 1)
 
-    def half(q):
-        return pl.ds(q * SUB, SUB)
-
-    def copy_a(st, q, t, slot):
+    both = pl.ds(0, 2)
+    parts_a = (((both, pl.ds(0, 2)), (both, pl.ds(2, 2))), ((pl.ds(0, 1), pl.ds(0, 4)), (pl.ds(1, 1), pl.ds(0, 2)), (pl.ds(1, 1), pl.ds(2, 2))))
+    parts_b = ((both, 0), (pl.ds(0, 1), 1), (pl.ds(1, 1), 1))
+
+    def copy_a(st, i, t, slot):
+        hs, ps = parts_a[st][i]
         return pltpu.make_async_remote_copy(
-            send_a.at[st, t, half(q)], recv_a.at[st, slot, half(q)], sem_as.at[st, q, t], sem_ar.at[st, q, slot],
+            send_a.at[st, t, hs, ps], recv_a.at[st, slot, hs, ps], sem_as.at[st, i, t], sem_ar.at[st, i, slot],
             device_id={"spec": t}, device_id_type=MESH,
         )
 
-    def copy_b(st, q, t, slot):
+    def copy_b(st, i, t, slot):
+        hs, q = parts_b[i]
         return pltpu.make_async_remote_copy(
-            send_b.at[st, t, half(q)], ren.at[st, slot, pl.ds(SUB + q * SUB, SUB)], sem_bs.at[st, q, t],
-            sem_br.at[st, q, slot], device_id={"spec": t}, device_id_type=MESH,
+            send_b.at[st, t, hs, pl.ds(2 * q, 2)], ren.at[st, slot, hs, pl.ds(2 + 2 * q, 2)], sem_bs.at[st, i, t],
+            sem_br.at[st, i, slot], device_id={"spec": t}, device_id_type=MESH,
         )
 
-    def copy_d(st, q, t, slot):
+    def copy_d(st, q, slot, t, key):
         return pltpu.make_async_remote_copy(
-            den_send.at[st, q], den.at[st, slot, 1 + q], sem_ds.at[st, q, t], sem_dr.at[st, q, slot],
+            den.at[st, slot, 1 + q], den.at[st, slot, 1 + q], sem_ds.at[st, q, key], sem_dr.at[st, q, slot],
             device_id={"spec": t}, device_id_type=MESH,
         )
 
-    def copy_h(st, q, y):
+    def start_d(st, q, dz):
+        for dx in (2, 1, 3):
+            copy_d(st, q, at(0, dz), at(dx, 0), at(dx, dz)).start()
+
+    def forward_d(st, q):
+        for dz in (1, 3, 2):
+            slot = at(0, dz)
+            copy_d(st, q, slot, slot, slot).wait_recv()
+            start_d(st, q, dz)
+
+    def copy_h(st, i, y):
+        hs, q = parts_b[i]
         return pltpu.make_async_remote_copy(
-            ren.at[st, y, pl.ds(SUB + q * SUB, SUB)], ren.at[st, y, pl.ds((1 - q) * (SUB + L), SUB)],
-            sem_hs.at[st, q, y], sem_hr.at[st, q, y],
+            ren.at[st, y, hs, pl.ds(2 + 2 * q, 2)], ren.at[st, y, hs, pl.ds(6 - 6 * q, 2)],
+            sem_hs.at[st, i, y], sem_hr.at[st, i, y],
             device_id={"slab": below if q else above}, device_id_type=MESH,
         )
 
@@ -123,17 +153,12 @@
             ))
         return out
 
-    for q in range(2):
-
-        @pl.loop(1, N + 1)
-        def _(d):
-            t = lax.rem(me + d, N)
-            for l in range(q * SUB, q * SUB + SUB):
-                send_a[0, t, l] = c32[pl.ds(l * Y + t, SP, stride=L * Y), :].astype(bf16)
-
-            @pl.when(d < N)
-            def _():
-                copy_a(0, q, t, me).start()
+    def start_a(st, i):
+        for t in partners:
+            copy_a(st, i, t, me).start()
+
+    start_a(0, 0)
+    start_a(0, 1)
 
     for cp in loads[1:]:
         cp.wait()
@@ -218,25 +243,23 @@
     def react(st, q):
         @pl.loop(q * SUB // 2, (q + 1) * SUB // 2)
         def _(p):
-            def both(a):
+            def twice(a):
                 return jnp.concatenate([a, a], axis=1)
 
-            def band(l):
-                return recv_a[st, :, l].reshape(S, X)
-
             l0 = 2 * p
-            gathered = jnp.concatenate([band(l0), band(l0 + 1)], axis=1)
+            pairs = recv_a[st, :, :, p].astype(f32).reshape(N, 2, 2, 8, X)
+            dissolved = jnp.concatenate([pairs[:, :, i].reshape(S, X) for i in range(2)], axis=1)
+            gathered = dissolved.astype(bf16)
             inhibition = jnp.dot(inhibit_ref[...], gathered, preferred_element_type=f32)
             boost = jnp.dot(priming_ref[...], gathered, preferred_element_type=f32)
-            dissolved = gathered.astype(f32)
-            rate = both(mr[...]) * (1.0 + boost) / (both(hs[...]) + dissolved + inhibition)
+            rate = twice(mr[...]) * (1.0 + boost) / (twice(hs[...]) + dissolved + inhibition)
             remaining = dissolved * jnp.exp(-rate)
             consumed = (dissolved - remaining).astype(bf16)
             roots = jnp.concatenate([root_b[pl.ds(l0, 1), :], root_b[pl.ds(l0 + 1, 1), :]], axis=1)
             reacted = (
                 remaining
                 + jnp.dot(produce_ref[...], consumed, preferred_element_type=f32)
-                + both(ex[...]) * jnp.broadcast_to(roots, (S, 2 * X))
+                + twice(ex[...]) * jnp.broadcast_to(roots, (S, 2 * X))
             )
             renewed = reacted.astype(bf16)
             low = (reacted - renewed.astype(f32)).astype(bf16)
@@ -250,70 +273,93 @@
                 hit = jnp.broadcast_to(labels, (M, X)) == lax.broadcasted_iota(jnp.int32, (M, X), 0)
                 d = 1.0 + jnp.sum(jnp.where(hit, sums[:, cols], 0.0), axis=0, keepdims=True)
                 den_send[st, q, pl.ds(l0 - q * SUB + i, 1), :] = d
-                send_b[st, :, l0 + i] = renewed[:, cols].reshape(N, SP, X)
-
-    def prep(st, es, rim):
-        @pl.loop(0, Y)
-        def _(y):
+            split = [reacted[:, i * X : (i + 1) * X].reshape(N, 2, 1, 8, X) for i in range(2)]
+            send_b[st, :, :, p] = jnp.concatenate(split, axis=2).reshape(N, 2, SP, X).astype(bf16)
+
+    def prep(st, h, pairs, rim):
+        rows = pl.ds(8 * h, 8)
+
+        @pl.loop(0, Y // 2)
+        def _(j):
             vals = []
-            for e in es:
-                r = ren[st, y, e].astype(f32)
-                d = jnp.broadcast_to(den[st, y, e // SUB, e % SUB : e % SUB + 1, :], (SP, X))
-                s = d / (d + ratio[y, e])
-                if rim:
-                    s = s * inside(e)
-                vals.append((r, s))
-            for e, (r, s) in zip(es, vals):
-                fld[y, e] = r
-                share[y, e] = s
-                mob[0][y + 1, e] = s * r
-
-    def substep(k, spans, rows, finish=None):
-        last = k == SUB - 1
-        halves = (pl.ds(0, 8), pl.ds(8, 8))
-
-        def span(y, es):
-            a = es[0]
-            cen = [mob[k][y + 1, a, h, :] for h in halves]
-            prev = [mob[k][y + 1, a - 1, h, :] for h in halves]
-            czp, vp = cz[y, a - 1], vz[y, a - 1]
-            fzp = [czp * (cen[i] - prev[i]) for i in range(2)]
-            wp = [vp * prev[i] for i in range(2)]
-            done = []
-            for e in es:
-                cze, ve = cz[y, e], vz[y, e]
-                xr, xl, n_, s_, dg = cxr[y, e], cxl[y, e], fy[y, e], fy[y + 1, e], diag[y, e]
-                for i, h in enumerate(halves):
-                    m = cen[i]
-                    nxt = mob[k][y + 1, e + 1, h, :]
-                    fz = cze * (nxt - m)
-                    w = ve * m
-                    acc = fz - fzp[i]
-                    acc += xr * pltpu.roll(m, X - 1, 1) + xl * pltpu.roll(m, 1, 1)
-                    acc += n_ * mob[k][y, e, h, :] + s_ * mob[k][y + 2, e, h, :]
-                    acc -= dg * m
-                    done.append(fld[y, e, h, :] + (wp[i] - w) + dif_h[i] * acc)
-                    cen[i], fzp[i], wp[i] = nxt, fz, w
-            if last:
-                for i, e in enumerate(es):
-                    finish(y, e - SUB, jnp.concatenate(done[2 * i : 2 * i + 2], axis=0))
+            for y in (2 * j, 2 * j + 1):
+                for pair in pairs:
+                    r2 = ren[st, y, h, pair].astype(f32)
+                    for i in range(2):
+                        e = 2 * pair + i
+                        r = r2[8 * i : 8 * i + 8]
+                        d = jnp.broadcast_to(den[st, y, e // SUB, e % SUB : e % SUB + 1, :], (8, X))
+                        s = d / (d + ratio[y, e, rows, :])
+                        if rim:
+                            s = s * inside(e)
+                        vals.append((y, e, r, s))
+            for y, e, r, s in vals:
+                fld[y, e, rows, :] = r
+                share[y, e, rows, :] = s
+                mob[0][y + 1, e, rows, :] = s * r
+
+    def substep(k, h, spans, n, finish=None):
+        hr = pl.ds(8 * h, 8)
+        src = mob[k]
+
+        @pl.loop(0, Y // n)
+        def _(j):
+            y0 = j * n
+            for es in spans:
+                a = es[0]
+                cen = [src[y0 + 1 + i, a, hr, :] for i in range(n)]
+                prev = [src[y0 + 1 + i, a - 1, hr, :] for i in range(n)]
+                fzp = [cz[y0 + i, a - 1] * (cen[i] - prev[i]) for i in range(n)]
+                wp = [vz[y0 + i, a - 1] * prev[i] for i in range(n)]
+                before = None
+                for e in es:
+                    rows = [src[y0, e, hr, :]] + cen + [src[y0 + n + 1, e, hr, :]]
+                    fyv = [fy[y0 + i, e] for i in range(n + 1)]
+                    nxt = [src[y0 + 1 + i, e + 1, hr, :] for i in range(n)]
+                    done = []
+                    for i in range(n):
+                        y, m = y0 + i, cen[i]
+                        fz = cz[y, e] * (nxt[i] - m)
+                        w = vz[y, e] * m
+                        acc = fz - fzp[i]
+                        acc += cxr[y, e] * pltpu.roll(m, X - 1, 1) + cxl[y, e] * pltpu.roll(m, 1, 1)
+                        acc += fyv[i] * rows[i] + fyv[i + 1] * rows[i + 2]
+                        acc -= diag[y, e] * m
+                        f = fld[y, e, hr, :] + (wp[i] - w) + dif_h[h] * acc
+                        fzp[i], wp[i] = fz, w
+                        if finish is None:
+                            fld[y, e, hr, :] = f
+                            mob[k + 1][y + 1, e, hr, :] = share[y, e, hr, :] * f
+                        else:
+                            done.append(f)
+                    cen = nxt
+                    if finish is not None:
+                        if e % 2:
+                            for i in range(n):
+                                finish(y0 + i, e - 1 - SUB, before[i], done[i])
+                        before = done
+
+    def own_part(st, h):
+        prep(st, h, range(2, 6), False)
+        for k in range(SUB - 1):
+            substep(k, h, [range(SUB + 1 + k, SUB + L - 1 - k)], (8, 16, 16)[k])
+
+    def rest(st, h):
+        prep(st, h, (0, 1, 6, 7), True)
+        for k in range(SUB - 1):
+            substep(k, h, [range(k + 1, SUB + 1 + k), range(SUB + L - 1 - k, E - 1 - k)], 8)
+
+        def finish(y, l, f0, f1):
+            if st < STEPS - 1:
+                send_a[st + 1, y, h, l // 2] = jnp.concatenate([f0, f1], axis=0).astype(bf16)
             else:
-                out = [share[y, e, h, :] for e in es for h in halves]
-                out = [a * b for a, b in zip(out, done)]
-                for i, e in enumerate(es):
-                    for n, h in enumerate(halves):
-                        fld[y, e, h, :] = done[2 * i + n]
-                        mob[k + 1][y + 1, e, h, :] = out[2 * i + n]
-
-        @pl.loop(0, Y // rows)
-        def _(j):
-            ys = [lax.rem(me + j * rows + 1 + i, N) for i in range(rows)]
-            for y in ys:
-                for es in spans:
-                    span(y, es)
-            if last:
-                for i, y in enumerate(ys):
-                    finish(y, None, j * rows + 1 + i)
+                for i, f in enumerate((f0, f1)):
+                    outs[pl.ds(pl.multiple_of((l + i) * Y * SP + y * SP + 8 * h, 8), 8), :] = f
+
+        for q in range(2):
+            substep(SUB - 1, h, [range(SUB + q * SUB, SUB + (q + 1) * SUB)], 8, finish)
+            if st < STEPS - 1 and (h or q):
+                start_a(st + 1, h * (1 + q))
 
     for st in range(STEPS):
         recv_a[st, me] = send_a[st, me]
@@ -322,34 +368,54 @@
             @pl.loop(1, N)
             def _(d):
                 src = lax.rem(me + N - d, N)
-                copy_a(st, q, src, src).wait_recv()
+                if st and q == 0:
+                    copy_a(st, 0, src, src).wait_recv()
+                copy_a(st, q + st, src, src).wait_recv()
 
             react(st, q)
 
-            @pl.loop(1, N)
-            def _(d):
-                t = lax.rem(me + d, N)
-                copy_d(st, q, t, me).start()
+            den[st, me, 1 + q] = den_send[st, q]
+            if q:
+                forward_d(st, 0)
+            for dz in (2, 1, 3):
+                t = at(0, dz)
+                copy_d(st, q, me, t, t).start()
+            start_d(st, q, 0)
+            for t in partners:
                 copy_b(st, q, t, me).start()
-
-            ren[st, me, pl.ds(SUB + q * SUB, SUB)] = send_b[st, me, half(q)]
-            den[st, me, 1 + q] = den_send[st, q]
+            ren[st, me, :, pl.ds(2 + 2 * q, 2)] = send_b[st, me, :, pl.ds(2 * q, 2)]
             copy_h(st, q, me).start()
 
+        for t in partners:
+            copy_b(st, 2, t, me).start()
+        copy_h(st, 2, me).start()
         for q in range(2):
 
             @pl.loop(1, N)
             def _(d):
                 src = lax.rem(me + N - d, N)
-                copy_d(st, q, src, src).wait_recv()
                 copy_b(st, q, src, src).wait_recv()
                 copy_h(st, q, src).start()
 
+            if q == 0:
+                forward_d(st, 1)
+
+        for q in range(2):
+
+            @pl.loop(4, N)
+            def _(d):
+                slot = lax.rem(x + d // 4, 4) * 4 + lax.rem(d, 4)
+                copy_d(st, q, slot, slot, slot).wait_recv()
+
             copy_g(st, q).start()
 
-        prep(st, range(SUB, SUB + L), False)
-        for k in range(SUB - 1):
-            substep(k, [range(SUB + 1 + k, SUB + L - 1 - k)], (4, 8, 16)[k])
+        own_part(st, 0)
+
+        @pl.loop(1, N)
+        def _(d):
+            src = lax.rem(me + N - d, N)
+            copy_b(st, 2, src, src).wait_recv()
+            copy_h(st, 2, src).start()
 
         for q in range(2):
             copy_g(st, q).wait_recv()
@@ -358,28 +424,14 @@
             def _(y):
                 copy_h(st, q, y).wait_recv()
 
-        prep(st, [*range(0, SUB), *range(SUB + L, E)], True)
-        for k in range(SUB - 1):
-            substep(k, [range(k + 1, SUB + 1 + k), range(SUB + L - 1 - k, E - 1 - k)], 4)
-        for q in range(2):
-            if st < STEPS - 1:
-
-                def finish(y, l, f):
-                    if l is not None:
-                        send_a[st + 1, y, l] = f.astype(bf16)
-                    else:
-
-                        @pl.when(f < N)
-                        def _():
-                            copy_a(st + 1, q, y, me).start()
-
-            else:
-
-                def finish(y, l, f):
-                    if l is not None:
-                        outs[pl.ds(pl.multiple_of(l * Y * SP + y * SP, SP), SP), :] = f
-
-            substep(SUB - 1, [range(SUB + q * SUB, SUB + (q + 1) * SUB)], 8, finish)
+        rest(st, 0)
+        own_part(st, 1)
+
+        @pl.loop(0, Y)
+        def _(y):
+            copy_h(st, 2, y).wait_recv()
+
+        rest(st, 1)
 
     @pl.loop(0, SP)
     def _(s):
@@ -389,19 +441,23 @@
     for cp in rims:
         cp.wait_send()
     for st in range(STEPS):
+
+        @pl.loop(1, N)
+        def _(d):
+            t = lax.rem(me + d, N)
+            for i in range(len(parts_a[st])):
+                copy_a(st, i, t, me).wait_send()
+            for i in range(3):
+                copy_b(st, i, t, me).wait_send()
+            for q in range(2):
+                copy_d(st, q, t, t, t).wait_send()
+
+        @pl.loop(0, Y)
+        def _(y):
+            for i in range(3):
+                copy_h(st, i, y).wait_send()
+
         for q in range(2):
-
-            @pl.loop(1, N)
-            def _(d):
-                t = lax.rem(me + d, N)
-                copy_a(st, q, t, me).wait_send()
-                copy_d(st, q, t, me).wait_send()
-                copy_b(st, q, t, me).wait_send()
-
-            @pl.loop(0, Y)
-            def _(y):
-                copy_h(st, q, y).wait_send()
-
             copy_g(st, q).wait_send()
 
 
@@ -427,10 +483,10 @@
             pltpu.VMEM((L, Y, X), jnp.int32),
             dma((14,)),
             pltpu.VMEM((SP * L * Y, X), f32),
-            pltpu.VMEM((STEPS, N, L, SP, X), bf16),
-            pltpu.VMEM((STEPS, N, L, SP, X), bf16),
-            pltpu.VMEM((STEPS, N, L, SP, X), bf16),
-            pltpu.VMEM((STEPS, Y, E, SP, X), bf16),
+            pltpu.VMEM((STEPS, N, 2, L // 2, SP, X), bf16),
+            pltpu.VMEM((STEPS, N, 2, L // 2, SP, X), bf16),
+            pltpu.VMEM((STEPS, N, 2, L // 2, SP, X), bf16),
+            pltpu.VMEM((STEPS, Y, 2, E // 2, SP, X), bf16),
             pltpu.VMEM((STEPS, 2, SUB, X), f32),
             pltpu.VMEM((STEPS, Y, 4, SUB, X), f32),
             pltpu.VMEM((E, Y, X), jnp.int32),
@@ -453,10 +509,10 @@
             pltpu.VMEM(big, f32),
             *[pltpu.VMEM((Y + 2, E, SP, X), f32)] * SUB,
             pltpu.VMEM((L * Y * SP, X), f32),
+            dma((STEPS, 3, N)), dma((STEPS, 3, N)),
+            dma((STEPS, 3, N)), dma((STEPS, 3, N)),
             dma((STEPS, 2, N)), dma((STEPS, 2, N)),
-            dma((STEPS, 2, N)), dma((STEPS, 2, N)),
-            dma((STEPS, 2, N)), dma((STEPS, 2, N)),
-            dma((STEPS, 2, Y)), dma((STEPS, 2, Y)),
+            dma((STEPS, 3, Y)), dma((STEPS, 3, Y)),
             dma((STEPS, 2)), dma((STEPS, 2)),
             dma((4,)), dma((4,)),
         ],

time: 103 us -> 100 us (0.971)
  Pallas kernels: 101 us -> 96.9 us
    pallas_call x1, Pallas kernels: 101 us -> 96.9 us  [body(): pl.pallas_call(kernel, out_shape=jax.ShapeDtypeStruct((SP, L, Y, X), bf16...]
where the time goes in v3:
time: 100 us; the launch traced here: 98.8 us
  Pallas kernels  96.9 us (97%)
  local copies, waits for them, and re-layouts  1.89 us (2%)
    pallas_call x1, Pallas kernels, body(): pl.pallas_call(kernel, out_shape=jax.ShapeDtypeStruct((SP, L, Y, X), bf16...  96.9 us

profile of v3, /device:TPU:16, one launch (start us, length us, event | category | flops | bytes accessed | tf_op | source)
XLA Modules:
  0.0 98.8 jit_solution(515041390513310984)
XLA Ops:
  0.0 96.9 %shard_map.136 = bf16[16,8,16,128]{3,2,1,0:T(8,128)(2,1)} custom-call(bf16[16,8,16,128]{3,2,1,0:T(8,128)(2,1)} %c_hbm.1, bf16[256,256]{1,0:T(8,128)(2,1)} %inhibit_hbm.1, bf16[256,256]{1,0:T(8,128)(2,1)} %priming_hbm.1, bf16[256,256]{1,0:T(8,128)(2,1)} %produce_hbm.1, f32[1,256]{1,0:T(1,128)} %bitcast.5, f32[1,256]{1,0:T(1,128)} %bitcast.6, ...), custom_call_target="tpu_custom_call" | custom-call | tf_op jit(solution)/shard_map/pallas_call | solution.py:472
  96.9 1.9 %copy.16 = bf16[16,8,16,128]{3,2,1,0:T(8,128)(2,1)} copy(bf16[16,8,16,128]{3,2,1,0:T(8,128)(2,1)} %shard_map.136) | data formatting | bytes 1048576

commit v4 on v3

--- a/solution.py
+++ b/solution.py
@@ -417,6 +417,8 @@
             copy_b(st, 2, src, src).wait_recv()
             copy_h(st, 2, src).start()
 
+        own_part(st, 1)
+
         for q in range(2):
             copy_g(st, q).wait_recv()
 
@@ -425,7 +427,6 @@
                 copy_h(st, q, y).wait_recv()
 
         rest(st, 0)
-        own_part(st, 1)
 
         @pl.loop(0, Y)
         def _(y):

time: 100 us -> 98.3 us (0.983)
  Pallas kernels: 96.9 us -> 94.9 us
    pallas_call x1, Pallas kernels: 96.9 us -> 94.9 us  [body(): pl.pallas_call(kernel, out_shape=jax.ShapeDtypeStruct((SP, L, Y, X), bf16...]
where the time goes in v4:
time: 98.3 us; the launch traced here: 96.8 us
  Pallas kernels  94.9 us (97%)
  local copies, waits for them, and re-layouts  1.89 us (2%)
    pallas_call x1, Pallas kernels, body(): pl.pallas_call(kernel, out_shape=jax.ShapeDtypeStruct((SP, L, Y, X), bf16...  94.9 us

profile of v4, /device:TPU:16, one launch (start us, length us, event | category | flops | bytes accessed | tf_op | source)
XLA Modules:
  0.0 96.8 jit_solution(16412419299526557463)
XLA Ops:
  0.0 94.9 %shard_map.136 = bf16[16,8,16,128]{3,2,1,0:T(8,128)(2,1)} custom-call(bf16[16,8,16,128]{3,2,1,0:T(8,128)(2,1)} %c_hbm.1, bf16[256,256]{1,0:T(8,128)(2,1)} %inhibit_hbm.1, bf16[256,256]{1,0:T(8,128)(2,1)} %priming_hbm.1, bf16[256,256]{1,0:T(8,128)(2,1)} %produce_hbm.1, f32[1,256]{1,0:T(1,128)} %bitcast.5, f32[1,256]{1,0:T(1,128)} %bitcast.6, ...), custom_call_target="tpu_custom_call" | custom-call | tf_op jit(solution)/shard_map/pallas_call | solution.py:473
  95.0 1.9 %copy.16 = bf16[16,8,16,128]{3,2,1,0:T(8,128)(2,1)} copy(bf16[16,8,16,128]{3,2,1,0:T(8,128)(2,1)} %shard_map.136) | data formatting | bytes 1048576
